TPU v7x, 1024 devices: a whole 4x8x16 slice. The times are simulated.
1024 devices in a mesh: dp: 16 (over y, core), emb: 64 (over x, z).
Axes of the slice: x: 4, y: 8, z: 16, core: 2. Of those that a mesh axis runs over, the one named last changes fastest.
Arguments:
- table: bfloat16 [32768, 512], P('emb'), may hold values from -6 to 6
- item_shard: int32 [262144, 1], P(('dp', 'emb')), may hold values from 0 to 63; in each aligned block of 256 rows (0 to 255, 256 to 511, ...) at most 8 rows name the same one
- item_row: int32 [262144], P(('dp', 'emb')), may hold values from 0 to 511
- segment_ids: int32 [1024, 256], P(('dp', 'emb')), may hold values from 0 to 15, never falling along the last dimension, each value on 1 to 128 neighbouring positions
- grad_out: bfloat16 [262144, 512], P(('dp', 'emb')), may hold values from -6 to 6
- w_in: bfloat16 [512, 2048], replicated, may hold values from -0.25 to 0.25
- w_out: bfloat16 [512, 512], replicated, may hold values from -0.25 to 0.25
Outputs:
- mixed: bfloat16 [262144, 512], P(('dp', 'emb'))
- table_grad: float32 [32768, 512], P(('emb', 'dp'))
Inputs may be any that keep to these rules, and one draw needn't show every extreme that they name: `item_shard`: at most 8 tokens of one device name one table shard; in every draw some device has exactly 8 tokens for some shard. `segment_ids`: within each row never falling; each of the 16 histories has 1 to 128 tokens, one exactly 128.
All inputs are finite; a program needn't handle non-finite values.
Results may differ from a plain program's by a relative error of at most 0.022.
Values may be sent and summed in bfloat16 or wider, within the bound.
A program may use at most 32 MiB of HBM per device.

v0:
```python
import jax
import jax.numpy as jnp
from jax import lax
from jax.sharding import PartitionSpec as P

HEADS = 8
MOST = 128


def layer(x, seg, w_in, w_out):
    length, width = x.shape
    proj = jax.nn.silu(jnp.dot(x, w_in, preferred_element_type=jnp.float32)).astype(jnp.bfloat16)
    u_part, v_part, q_part, k_part = jnp.split(proj, 4, axis=1)
    queries = q_part.reshape(length, HEADS, -1)
    keys_all = k_part.reshape(length, HEADS, -1)
    values = v_part.reshape(length, HEADS, -1)
    scores = jnp.einsum(
        "qhd,khd->hqk", queries, keys_all, preferred_element_type=jnp.float32
    ) * queries.shape[2] ** (-0.5)
    place = jnp.arange(length)
    causal = (place[None, :] <= place[:, None]) & (seg[:, None] == seg[None, :])
    weights = jnp.where(causal[None], jax.nn.silu(scores) / MOST, 0.0).astype(jnp.bfloat16)
    attended = jnp.einsum(
        "hqk,khd->qhd", weights, values, preferred_element_type=jnp.float32
    ).reshape(length, width)
    center = attended - jnp.mean(attended, axis=1, keepdims=True)
    normed = center * lax.rsqrt(jnp.mean(center * center, axis=1, keepdims=True) + 1e-05)
    gated = (normed * u_part.astype(jnp.float32)).astype(jnp.bfloat16)
    return (
        jnp.dot(gated, w_out, preferred_element_type=jnp.float32) + x.astype(jnp.float32)
    ).astype(jnp.bfloat16)


def body(table, item_shard, item_row, segment_ids, grad_out, w_in, w_out):
    groups = lax.axis_size("emb")
    count = item_row.shape[0]
    width = table.shape[1]
    rows_here = table.shape[0]
    slots = 2 * count // groups
    owner = item_shard[:, 0]
    onehot = (owner[:, None] == jnp.arange(groups, dtype=jnp.int32)[None, :]).astype(jnp.float32)
    earlier = jnp.dot(
        jnp.tri(count, k=-1, dtype=jnp.float32), onehot, precision=lax.Precision.HIGHEST
    )
    slot = jnp.sum(earlier * onehot, axis=1).astype(jnp.int32)
    target = owner * slots + slot
    requests = (
        jnp.full((groups * slots,), -1, jnp.int32).at[target].set(item_row).reshape(groups, slots)
    )
    asked = lax.all_to_all(requests, "emb", split_axis=0, concat_axis=0, tiled=True)
    fetched = jnp.where(
        (asked >= 0)[..., None], table[jnp.maximum(asked, 0)], jnp.zeros((), jnp.bfloat16)
    )
    returned = lax.all_to_all(fetched, "emb", split_axis=0, concat_axis=0, tiled=True)
    returned, asked = (returned, asked)
    embedded = returned.reshape(groups * slots, width)[target]
    mixed, pull = jax.vjp(lambda inputs: layer(inputs, segment_ids[0], w_in, w_out), embedded)
    (d_embedded,) = pull(grad_out)
    outgoing = (
        jnp.zeros((groups * slots, width), jnp.bfloat16)
        .at[target]
        .set(d_embedded)
        .reshape(groups, slots, width)
    )
    incoming, row_numbers = (
        lax.all_to_all(outgoing, "emb", split_axis=0, concat_axis=0, tiled=True),
        lax.all_to_all(requests, "emb", split_axis=0, concat_axis=0, tiled=True),
    )
    flat_ids = row_numbers.reshape(-1)
    placed = jnp.where(flat_ids >= 0, flat_ids, rows_here)
    dense = (
        jnp.zeros((rows_here, width), jnp.float32)
        .at[placed]
        .add(incoming.reshape(-1, width).astype(jnp.float32), mode="drop")
    )
    totals = lax.psum(dense.astype(jnp.bfloat16), "dp").astype(jnp.float32)
    piece = rows_here // lax.axis_size("dp")
    table_grad = lax.dynamic_slice_in_dim(totals, lax.axis_index("dp") * piece, piece, 0)
    return (mixed, table_grad)


def solution(mesh):
    return jax.shard_map(
        body,
        mesh=mesh,
        in_specs=(
            P("emb", None),
            P(("dp", "emb"), None),
            P(("dp", "emb")),
            P(("dp", "emb"), None),
            P(("dp", "emb"), None),
            P(),
            P(),
        ),
        out_specs=(P(("dp", "emb"), None), P(("emb", "dp"), None)),
        check_vma=False,
    )
```

profile of v0, /device:TPU:1, one launch (start us, length us, event | category | flops | bytes accessed | tf_op | source)
XLA Modules:
  0.0 285.5 jit_solution(14010828196374995290)
XLA Ops:
  7.2 0.0 copy-start
  7.2 1.1 fusion.16
  8.3 0.7 compare_select_fusion.2
  9.0 1.6 scatter_custom_fusion
  10.6 0.1 all_to_all.13
  10.7 35.9 %all_to_all.20 = s32[64,1,8]{2,1,0:T(1,128)S(1)} all-to-all(s32[64,1,8]{2,1,0:T(1,128)S(1)} %bitcast.76), channel_id=1, replica_groups=mesh['dp'=16,'emb'=64] {'emb'}, dimensions={0} | all-to-all | bytes 4096 | tf_op jit(solution)/shard_map/all_to_all | solution.py:50
  46.5 0.1 copy.38
  46.6 0.1 copy.39
  46.7 0.1 copy.41
  46.8 0.1 reshape.186
  46.9 3.1 %gather_fusion = bf16[512,512]{1,0:T(8,128)(2,1)S(1)} fusion(bf16[512,512]{1,0:T(8,128)(2,1)} %param.7, s32[1024]{0:T(1024)S(1)} %pad_clamp_fusion.1), kind=kCustom, calls=%fused_computation | custom fusion | bytes 1050624 | tf_op jit(solution)/shard_map/gather | solution.py:52
  50.0 0.0 copy-start.13
  50.0 0.9 bitcast_select_fusion
  50.9 4.8 %all-to-all-start.1 = ((bf16[64,8,512]{2,1,0:T(8,128)(2,1)}), bf16[64,8,512]{2,1,0:T(8,128)(2,1)S(1)}, u32[]{:S(2)}, u32[]{:S(2)}) async-start(bf16[64,8,512]{2,1,0:T(8,128)(2,1)} %bitcast_select_fusion), calls=%async_computation.1 | async-start | bytes 1048576 | tf_op jit(solution)/shard_map/all_to_all | solution.py:54
  55.8 0.0 copy-done.13
  55.8 0.1 fusion.37
  55.9 27.6 %all-to-all-done.1 = bf16[64,8,512]{2,1,0:T(8,128)(2,1)S(1)} async-done(((bf16[64,8,512]{2,1,0:T(8,128)(2,1)}), bf16[64,8,512]{2,1,0:T(8,128)(2,1)S(1)}, u32[]{:S(2)}, u32[]{:S(2)}) %all-to-all-start.1) | async-done | bytes 524320 | tf_op jit(solution)/shard_map/all_to_all | solution.py:54
  83.5 1.2 gather_fusion.1
  84.7 0.0 copy-done
  84.7 0.0 copy-start.4
  84.7 2.1 multiply_convert_fusion
  86.8 0.0 copy-done.4
  86.8 1.0 copy-done.2
  87.7 0.1 fusion.47
  87.8 0.1 copy.44
  87.9 0.0 copy-start.6
  88.0 0.1 copy.43
  88.1 0.0 copy-start.8
  88.1 0.1 copy.42
  88.2 2.2 select_convert_fusion
  90.4 0.0 copy-done.6
  90.4 0.0 copy-done.8
  90.4 0.5 fusion.48
  90.9 0.1 fusion.30
  91.0 0.4 copy-done.1
  91.4 0.2 copy.45
  91.6 1.6 multiply_reduce_fusion
  93.3 1.9 fusion.46
  95.2 0.1 broadcast_add_fusion
  95.3 0.1 copy.46
  95.5 2.3 fusion.51
  97.8 3.0 %fusion.7 = bf16[8,256,256]{2,1,0:T(8,128)(2,1)S(1)} fusion(f32[8,256,256]{2,1,0:T(8,128)} %get-tuple-element.13, bf16[8,64,256]{2,1,0:T(8,128)(2,1)} %bitcast.74, bf16[256,8,64]{0,2,1:T(8,128)(2,1)S(1)} %bitcast.66, pred[256,256]{1,0:T(8,128)(4,1)S(1)} %fusion.37), kind=kOutput, calls=%fused_computation.14 | convolution fusion | flops 74973184 | bytes 3735552 | tf_op jit(solution)/shard_map/transpose(jvp(hqk,khd->qhd))/dot_general | solution.py:23
  100.9 1.0 fusion.49
  101.9 1.1 fusion.50
  103.0 0.1 copy.47
  103.2 1.1 copy.48
  104.3 0.0 copy-done.11
  104.3 0.9 copy.49
  105.2 2.8 fusion.13
  107.9 2.3 scatter_custom_fusion.1
  110.2 10.0 %all-to-all-start.2 = ((bf16[64,8,512]{2,1,0:T(8,128)(2,1)}), bf16[64,8,512]{2,1,0:T(8,128)(2,1)}, u32[]{:S(2)}, u32[]{:S(2)}) async-start(bf16[64,8,512]{2,1,0:T(8,128)(2,1)} %bitcast.23), calls=%async_computation.2 | async-start | bytes 1048576 | tf_op jit(solution)/shard_map/all_to_all | solution.py:66
  120.2 0.0 copy-start.3
  120.2 0.0 copy-start.5
  120.2 0.3 all-reduce.2.cloned.1.call-start
  120.5 0.5 broadcast.174
  121.0 0.7 reduce.6
  121.8 0.1 reshape.177
  121.9 26.1 %all-to-all-done.2 = bf16[64,8,512]{2,1,0:T(8,128)(2,1)} async-done(((bf16[64,8,512]{2,1,0:T(8,128)(2,1)}), bf16[64,8,512]{2,1,0:T(8,128)(2,1)}, u32[]{:S(2)}, u32[]{:S(2)}) %all-to-all-start.2) | async-done | bytes 524320 | tf_op jit(solution)/shard_map/all_to_all | solution.py:66
  148.0 5.1 %scatter_custom_fusion.2 = f32[512,512]{1,0:T(8,128)} fusion(s32[512]{0:T(512)S(1)} %bitcast.82, bf16[64,8,512]{2,1,0:T(8,128)(2,1)} %all-to-all-done.2, f32[]{:T(128)} %constant.17.clone.1), kind=kCustom, calls=%fused_computation.38 | custom fusion | flops 524288 | bytes 1572868 | tf_op jit(solution)/shard_map/scatter-add | solution.py:74
  153.1 2.1 convert_element_type.109
  155.2 0.0 all-reduce.2.cloned.1.call-update
  155.2 2.0 fusion.8
  157.3 120.0 %all-reduce.2.cloned.1.call-done = bf16[512,512]{1,0:T(8,128)(2,1)} async-done(((bf16[512,512]{1,0:T(8,128)(2,1)}), bf16[512,512]{1,0:T(8,128)(2,1)}) %all-reduce.2.cloned.1.call-update) | async-done | bytes 524304 | tf_op jit(solution)/shard_map/psum | solution.py:76
  277.3 1.4 dynamic-slice_convert_fusion
  (23 shorter events, 0.1 us)
Async XLA Ops:
  7.2 77.5 %copy-start = (bf16[512,2048]{1,0:T(8,128)(2,1)S(1)}, bf16[512,2048]{1,0:T(8,128)(2,1)}, u32[]{:S(2)}) copy-start(bf16[512,2048]{1,0:T(8,128)(2,1)} %param.12) | copy-start | bytes 6291460
  50.0 5.8 %copy-start.13 = (s32[1,256]{1,0:T(1,128)S(1)}, s32[1,256]{1,0:T(1,128)}, u32[]{:S(2)}) copy-start(s32[1,256]{1,0:T(1,128)} %param.10) | copy-start | bytes 3076
  50.9 32.6 %all-to-all-start.1 = ((bf16[64,8,512]{2,1,0:T(8,128)(2,1)}), bf16[64,8,512]{2,1,0:T(8,128)(2,1)S(1)}, u32[]{:S(2)}, u32[]{:S(2)}) async-start(bf16[64,8,512]{2,1,0:T(8,128)(2,1)} %bitcast_select_fusion), calls=%async_computation.1 | async-start | bytes 1048576 | tf_op jit(solution)/shard_map/all_to_all | solution.py:54
  84.7 2.1 copy-start.4
  86.8 1.0 copy-start.2
  87.9 2.5 copy-start.6
  88.1 2.3 copy-start.8
  90.4 1.0 copy-start.1
  95.5 2.3 copy-start.12
  97.8 3.0 %copy-start.9 = (bf16[256,512]{0,1:T(8,128)(2,1)S(1)}, bf16[256,512]{0,1:T(8,128)(2,1)}, u32[]{:S(2)}) copy-start(bf16[256,512]{0,1:T(8,128)(2,1)} %copy-done.8) | copy-start | bytes 786436
  97.8 4.1 %copy-start.7 = (bf16[256,512]{0,1:T(8,128)(2,1)S(1)}, bf16[256,512]{0,1:T(8,128)(2,1)}, u32[]{:S(2)}) copy-start(bf16[256,512]{0,1:T(8,128)(2,1)} %copy-done.6) | copy-start | bytes 786436
  100.9 2.2 copy-start.10
  101.9 2.4 copy-start.11
  110.2 37.7 %all-to-all-start.2 = ((bf16[64,8,512]{2,1,0:T(8,128)(2,1)}), bf16[64,8,512]{2,1,0:T(8,128)(2,1)}, u32[]{:S(2)}, u32[]{:S(2)}) async-start(bf16[64,8,512]{2,1,0:T(8,128)(2,1)} %bitcast.23), calls=%async_computation.2 | async-start | bytes 1048576 | tf_op jit(solution)/shard_map/all_to_all | solution.py:66
  120.2 35.0 %copy-start.3 = (bf16[512,512]{1,0:T(8,128)(2,1)S(1)}, bf16[512,512]{1,0:T(8,128)(2,1)}, u32[]{:S(2)}) copy-start(bf16[512,512]{1,0:T(8,128)(2,1)} %param.13) | copy-start | bytes 1572868
  120.2 35.0 %copy-start.5 = (bf16[256,512]{1,0:T(8,128)(2,1)S(1)}, bf16[256,512]{1,0:T(8,128)(2,1)}, u32[]{:S(2)}) copy-start(bf16[256,512]{1,0:T(8,128)(2,1)} %copy-done.4) | copy-start | bytes 786436
  120.2 157.0 %all-reduce.2.cloned.1.call-start = ((), (), s32[]{:S(2)}) async-start(), calls=%async_computation.3 | async-start | bytes 1048576 | tf_op jit(solution)/shard_map/psum | solution.py:76
Sparse Core Ops, SparseCore 0:
  155.3 121.8 all-reduce.1
where the time goes:
time: 286 us; the launch traced here: 285 us
  waiting for transfers between devices  174 us (61%)
  blocking collectives  35.9 us (13%)
  matrix products  19.8 us (7%)
  starting transfers between devices  15 us (5%)
  between operations  14.4 us (5%)
  local copies, waits for them, and re-layouts  13.5 us (5%)
  other arithmetic  13.3 us (5%)
    psum x1, waiting for transfers between devices, body(): totals = lax.psum(dense.astype(jnp.bfloat16), 'dp').astype(jnp.float32)  120 us
    all_to_all x1, blocking collectives, body(): lax.all_to_all(requests, 'emb', split_axis=0, concat_axis=0, tiled=True)  35.9 us
    all_to_all x1, waiting for transfers between devices, body(): lax.all_to_all(fetched, 'emb', split_axis=0, concat_axis=0, tiled=True)  27.6 us
    all_to_all x1, waiting for transfers between devices, body(): lax.all_to_all(outgoing, 'emb', split_axis=0, concat_axis=0, tiled=True)  26.1 us
    all_to_all x1, starting transfers between devices, body(): lax.all_to_all(outgoing, 'emb', split_axis=0, concat_axis=0, tiled=True)  9.96 us
    dot_general x3, matrix products, layer(): jnp.einsum('hqk,khd->qhd', weights, values, preferred_element_type=jnp.fl...  5.83 us
  transfers between devices with their start and end apart: 3, of which 3 were waited for; matrix products, arithmetic and copies ran while one was open for 1% of the time, Pallas kernels for 0%

commit v1 on v0

v1 whole, which is shorter than its diff:
```python
import functools

import jax
import jax.numpy as jnp
from jax import lax
from jax.experimental import pallas as pl
from jax.experimental.pallas import tpu as pltpu
from jax.sharding import PartitionSpec as P

HEADS = 8
CAP = 8
MOST = 128
MESH = pl.DeviceIdType.MESH
F32 = jnp.float32
BF16 = jnp.bfloat16


def dot(a, b, contract=(1, 0)):
    return lax.dot_general(
        a, b, (((contract[0],), (contract[1],)), ((), ())), preferred_element_type=F32
    )


def iota(shape, axis):
    return lax.broadcasted_iota(jnp.int32, shape, axis)


def to_col(row):
    n = row.shape[1]
    return jnp.sum(jnp.where(iota((n, n), 0) == iota((n, n), 1), row, 0.0), axis=1, keepdims=True)


def sigmoid(value):
    return 0.5 * jnp.tanh(0.5 * value) + 0.5


def near(step, size):
    return jnp.where(step % 2 == 1, (step + 1) // 2, size - step // 2)


def forward_backward(seg_row, x_ref, grad_ref, win_ref, wout_ref, mixed_ref, dx_ref,
                     proj_ref, slope_ref, weight_ref, wslope_ref, dz_ref):
    tokens, width = x_ref.shape
    pairs = HEADS // 2
    lanes = 2 * width // HEADS
    scale = (width // HEADS) ** -0.5

    def part(index):
        return slice(index * width, (index + 1) * width)

    x = x_ref[...]
    for index in range(4):
        z = dot(x, win_ref[:, part(index)])
        sig = sigmoid(z)
        act = z * sig
        proj_ref[:, part(index)] = act.astype(BF16)
        slope_ref[:, part(index)] = sig + act * (1.0 - sig)

    seg_col = to_col(seg_row)
    seen = (iota((tokens, tokens), 1) <= iota((tokens, tokens), 0)) & (seg_col == seg_row)
    factor = jnp.where(seen, 1.0 / MOST, 0.0)
    factor = jnp.concatenate([factor, factor], axis=0)
    first = iota((tokens, lanes), 1) < lanes // 2

    def stack(value):
        zero = jnp.zeros_like(value)
        return jnp.concatenate([jnp.where(first, value, zero), jnp.where(first, zero, value)], axis=0)

    def unstack(value):
        return jnp.where(first, value[:tokens], value[tokens:])

    def pair(index, which):
        start = which * width + index * lanes
        return slice(start, start + lanes)

    attended = []
    for index in range(pairs):
        q = stack(proj_ref[:, pair(index, 2)])
        s = dot(q, proj_ref[:, pair(index, 3)], (1, 1)) * scale
        sig = sigmoid(s)
        act = s * sig
        weights = (act * factor).astype(BF16)
        weight_ref[index] = weights
        wslope_ref[index] = (sig + act * (1.0 - sig)) * (factor * scale)
        attended.append(unstack(dot(weights, proj_ref[:, pair(index, 1)])))
    attended = jnp.concatenate(attended, axis=1)

    center = attended - jnp.mean(attended, axis=1, keepdims=True)
    rstd = lax.rsqrt(jnp.mean(center * center, axis=1, keepdims=True) + 1e-05)
    normed = center * rstd
    u = proj_ref[:, part(0)].astype(F32)
    gated = (normed * u).astype(BF16)
    mixed_ref[...] = (dot(gated, wout_ref[...]) + x.astype(F32)).astype(BF16)

    d_gated = dot(grad_ref[...], wout_ref[...], (1, 1)).astype(BF16).astype(F32)
    d_u = (d_gated * normed).astype(BF16).astype(F32)
    dz_ref[:, part(0)] = (d_u * slope_ref[:, part(0)]).astype(BF16)
    d_normed = d_gated * u
    d_att = rstd * (
        d_normed
        - jnp.mean(d_normed, axis=1, keepdims=True)
        - normed * jnp.mean(d_normed * normed, axis=1, keepdims=True)
    )
    d_att = d_att.astype(BF16)

    def put(index, which, value):
        value = value.astype(BF16).astype(F32)
        dz_ref[:, pair(index, which)] = (value * slope_ref[:, pair(index, which)]).astype(BF16)

    for index in range(pairs):
        q = stack(proj_ref[:, pair(index, 2)])
        d = stack(d_att[:, index * lanes:(index + 1) * lanes])
        put(index, 1, dot(weight_ref[index], d, (0, 0)))
        d_s = dot(d, proj_ref[:, pair(index, 1)], (1, 1)) * wslope_ref[index]
        d_s = d_s.astype(BF16)
        put(index, 2, unstack(dot(d_s, proj_ref[:, pair(index, 3)])))
        put(index, 3, dot(d_s, q, (0, 0)))

    d_x = dot(dz_ref[...], win_ref[...], (1, 1)).astype(BF16).astype(F32)
    dx_ref[...] = (d_x + grad_ref[...].astype(F32)).astype(BF16)


def kernel(nx, nz, nd, chunks,
           owner_ref, row_ref, seg_ref, table_hbm, grad_hbm, win_hbm, wout_hbm,
           mixed_ref, out_ref,
           table_ref, grad_ref, win_ref, wout_ref,
           ask_ref, mid_ref, comb_ref, fin_ref,
           place_ref, back_ref, put_ref,
           send_ref, recv_ref, x_ref, dx_ref,
           proj_ref, slope_ref, weight_ref, wslope_ref, dz_ref,
           gsend_ref, grecv_ref, dsend_ref, drecv_ref,
           load_sem, zs_sem, zr_sem, xs_sem, xr_sem, rs_sem, rr_sem, gs_sem, gr_sem, ds_sem, dr_sem):
    emb = lax.axis_index("emb")
    dp = lax.axis_index("dp")
    x_at, z_at = emb // nz, emb % nz
    groups = nx * nz
    tokens, width = x_ref.shape
    rows = table_ref.shape[0]
    lanes = nz * CAP
    half = width // (2 * chunks)

    loads = [
        pltpu.make_async_copy(source, target, load_sem.at[index])
        for index, (source, target) in enumerate(
            [(table_hbm, table_ref), (win_hbm, win_ref), (wout_hbm, wout_ref), (grad_hbm, grad_ref)]
        )
    ]
    for load in loads:
        load.start()

    barrier = pltpu.get_barrier_semaphore()

    def greet(step, carry):
        pl.semaphore_signal(barrier, 1, device_id={"emb": (emb + step) % groups}, device_id_type=MESH)
        return carry

    def greet_dp(step, carry):
        pl.semaphore_signal(barrier, 1, device_id={"dp": (dp + step) % nd}, device_id_type=MESH)
        return carry

    lax.fori_loop(1, groups, greet, 0)
    lax.fori_loop(1, nd, greet_dp, 0)

    def finish(ref, count, sem):
        pltpu.make_async_copy(ref.at[pl.ds(0, count)], ref.at[pl.ds(0, count)], sem).wait()

    owner = owner_ref[...].astype(F32)
    named = iota((groups, tokens), 0).astype(F32) == owner
    before = (iota((tokens, tokens), 0) < iota((tokens, tokens), 1)).astype(BF16)
    named_bf = named.astype(BF16)
    slot = jnp.sum(jnp.where(named, dot(named_bf, before), 0.0), axis=0, keepdims=True)
    target = owner * CAP + slot
    place_ref[...] = (to_col(target) == iota((tokens, groups * CAP), 1).astype(F32)).astype(BF16)
    back_ref[...] = (iota((groups * CAP, tokens), 0).astype(F32) == target).astype(BF16)
    number = to_col((row_ref[...] + 1).astype(F32))
    lane = to_col(slot) + (z_at * CAP).astype(F32)
    here = lane == iota((tokens, lanes), 1).astype(F32)
    high = jnp.floor(number * (1.0 / 16.0))
    low = number - 16.0 * high
    ask = 16.0 * dot(named_bf, jnp.where(here, high, 0.0).astype(BF16)) + dot(
        named_bf, jnp.where(here, low, 0.0).astype(BF16)
    )
    for at in range(nx):
        ask_ref[:, pl.ds(at, 1), :] = ask[at * nz:(at + 1) * nz].reshape(nz, 1, lanes)

    pl.semaphore_wait(barrier, groups + nd - 2)

    def ask_z(step, carry):
        peer = (z_at + near(step, nz)) % nz
        pltpu.make_async_remote_copy(
            src_ref=ask_ref.at[peer], dst_ref=mid_ref.at[z_at], send_sem=zs_sem, recv_sem=zr_sem,
            device_id={"emb": x_at * nz + peer}, device_id_type=MESH,
        ).start()
        return carry

    lax.fori_loop(1, nz, ask_z, 0)
    mid_ref[z_at] = ask_ref[z_at]
    finish(mid_ref, nz - 1, zr_sem)
    comb = jnp.sum(mid_ref[...], axis=0)
    for at in range(nx):
        comb_ref[at] = comb[at:at + 1]

    def ask_x(step, carry):
        peer = (x_at + step) % nx
        pltpu.make_async_remote_copy(
            src_ref=comb_ref.at[peer], dst_ref=fin_ref.at[x_at], send_sem=xs_sem, recv_sem=xr_sem,
            device_id={"emb": peer * nz + z_at}, device_id_type=MESH,
        ).start()
        return carry

    lax.fori_loop(1, nx, ask_x, 0)
    fin_ref[x_at] = comb_ref[x_at]
    finish(fin_ref, nx - 1, xr_sem)

    def send_group(first, at, source, target, send_sem, recv_sem):
        def send(step, carry):
            peer = at * nz + (z_at + near(step, nz)) % nz
            pltpu.make_async_remote_copy(
                src_ref=source.at[peer], dst_ref=target.at[emb], send_sem=send_sem, recv_sem=recv_sem,
                device_id={"emb": peer}, device_id_type=MESH,
            ).start()
            return carry

        lax.fori_loop(first, nz + first, send, 0) if first == 0 else lax.fori_loop(1, nz, send, 0)

    def blocks(value):
        left = value[:, :half].reshape(nz, CAP, half)
        right = value[:, half:].reshape(nz, CAP, half)
        return jnp.concatenate([left, right], axis=1).astype(BF16)

    def unblocks(value):
        value = value.astype(F32)
        left = value[:, :CAP].reshape(groups * CAP, half)
        right = value[:, CAP:].reshape(groups * CAP, half)
        return jnp.concatenate([left, right], axis=1).astype(BF16)

    loads[0].wait()

    def answer(step, first):
        at = (x_at + step) % nx
        asked = to_col(fin_ref[at])
        pick = (asked == (iota((lanes, rows), 1) + 1).astype(F32)).astype(BF16)
        for side in range(chunks):
            cols = slice(side * 2 * half, (side + 1) * 2 * half)
            send_ref[side, pl.ds(at * nz, nz)] = blocks(dot(pick, table_ref[:, cols]))
        for side in range(chunks):
            send_group(first, at, send_ref.at[side], recv_ref.at[side], rs_sem.at[side], rr_sem.at[side])

    answer(0, 1)

    def answer_other(step, carry):
        answer(step, 0)
        return carry

    lax.fori_loop(1, nx, answer_other, 0)
    for side in range(chunks):
        recv_ref[side, emb] = send_ref[side, emb]

    asked = jnp.concatenate([fin_ref[at] for at in range(nx)], axis=1)
    put_ref[...] = ((iota((rows, groups * CAP), 0) + 1).astype(F32) == asked).astype(BF16)

    for side in range(chunks):
        finish(recv_ref.at[side], groups - 1, rr_sem.at[side])
        cols = slice(side * 2 * half, (side + 1) * 2 * half)
        x_ref[:, cols] = dot(place_ref[...], unblocks(recv_ref[side])).astype(BF16)

    for load in loads[1:]:
        load.wait()
    forward_backward(seg_ref[...].astype(F32), x_ref, grad_ref, win_ref, wout_ref, mixed_ref, dx_ref,
                     proj_ref, slope_ref, weight_ref, wslope_ref, dz_ref)

    for side in range(chunks):
        cols = slice(side * 2 * half, (side + 1) * 2 * half)

        def give(step, first):
            at = (x_at + step) % nx
            mine = back_ref[pl.ds(pl.multiple_of(at * lanes, lanes), lanes), :]
            gsend_ref[side, pl.ds(at * nz, nz)] = blocks(dot(mine, dx_ref[:, cols]))
            send_group(first, at, gsend_ref.at[side], grecv_ref.at[side], gs_sem.at[side], gr_sem.at[side])

        give(0, 1)

        def give_other(step, carry):
            give(step, 0)
            return carry

        lax.fori_loop(1, nx, give_other, 0)
        grecv_ref[side, emb] = gsend_ref[side, emb]

    for side in range(chunks):
        finish(grecv_ref.at[side], groups - 1, gr_sem.at[side])
        dense = dot(put_ref[...], unblocks(grecv_ref[side]))
        dsend_ref[side] = dense.reshape(nd, rows // nd, 2 * half).astype(BF16)

        def send_dp(step, carry):
            peer = (dp + step) % nd
            pltpu.make_async_remote_copy(
                src_ref=dsend_ref.at[side, peer], dst_ref=drecv_ref.at[side, dp],
                send_sem=ds_sem.at[side], recv_sem=dr_sem.at[side],
                device_id={"dp": peer}, device_id_type=MESH,
            ).start()
            return carry

        lax.fori_loop(1, nd, send_dp, 0)
        drecv_ref[side, dp] = dsend_ref[side, dp]

    for side in range(chunks):
        finish(drecv_ref.at[side], nd - 1, dr_sem.at[side])
        cols = slice(side * 2 * half, (side + 1) * 2 * half)
        out_ref[:, cols] = jnp.sum(drecv_ref[side].astype(F32), axis=0)

    finish(ask_ref, nz - 1, zs_sem)
    finish(comb_ref, nx - 1, xs_sem)
    for side in range(chunks):
        finish(send_ref.at[side], groups - 1, rs_sem.at[side])
        finish(gsend_ref.at[side], groups - 1, gs_sem.at[side])
        finish(dsend_ref.at[side], nd - 1, ds_sem.at[side])


def layer(nx, nz, nd, table, item_shard, item_row, segment_ids, grad_out, w_in, w_out):
    tokens, width = grad_out.shape
    rows = table.shape[0]
    groups = nx * nz
    lanes = nz * CAP
    chunks = 1
    half = width // (2 * chunks)
    vmem = pl.BlockSpec(memory_space=pltpu.VMEM)
    anywhere = pl.BlockSpec(memory_space=pl.ANY)
    dma = pltpu.SemaphoreType.DMA
    pairs = HEADS // 2
    return pl.pallas_call(
        functools.partial(kernel, nx, nz, nd, chunks),
        out_shape=(
            jax.ShapeDtypeStruct((tokens, width), BF16),
            jax.ShapeDtypeStruct((rows // nd, width), F32),
        ),
        in_specs=[vmem] * 3 + [anywhere] * 4,
        out_specs=(vmem, vmem),
        scratch_shapes=[
            pltpu.VMEM((rows, width), BF16),
            pltpu.VMEM((tokens, width), BF16),
            pltpu.VMEM((width, 4 * width), BF16),
            pltpu.VMEM((width, width), BF16),
            pltpu.VMEM((nz, nx, lanes), F32),
            pltpu.VMEM((nz, nx, lanes), F32),
            pltpu.VMEM((nx, 1, lanes), F32),
            pltpu.VMEM((nx, 1, lanes), F32),
            pltpu.VMEM((tokens, groups * CAP), BF16),
            pltpu.VMEM((groups * CAP, tokens), BF16),
            pltpu.VMEM((rows, groups * CAP), BF16),
            pltpu.VMEM((chunks, groups, 2 * CAP, half), BF16),
            pltpu.VMEM((chunks, groups, 2 * CAP, half), BF16),
            pltpu.VMEM((tokens, width), BF16),
            pltpu.VMEM((tokens, width), BF16),
            pltpu.VMEM((tokens, 4 * width), BF16),
            pltpu.VMEM((tokens, 4 * width), F32),
            pltpu.VMEM((pairs, 2 * tokens, tokens), BF16),
            pltpu.VMEM((pairs, 2 * tokens, tokens), F32),
            pltpu.VMEM((tokens, 4 * width), BF16),
            pltpu.VMEM((chunks, groups, 2 * CAP, half), BF16),
            pltpu.VMEM((chunks, groups, 2 * CAP, half), BF16),
            pltpu.VMEM((chunks, nd, rows // nd, 2 * half), BF16),
            pltpu.VMEM((chunks, nd, rows // nd, 2 * half), BF16),
            dma((4,)), dma, dma, dma, dma,
            dma((chunks,)), dma((chunks,)), dma((chunks,)), dma((chunks,)), dma((chunks,)), dma((chunks,)),
        ],
        compiler_params=pltpu.CompilerParams(
            collective_id=0, has_side_effects=True, vmem_limit_bytes=48 * 2**20
        ),
        name="hstu",
    )(item_shard.reshape(1, tokens), item_row.reshape(1, tokens), segment_ids, table, grad_out, w_in, w_out)


def solution(mesh, nx=4):
    return jax.shard_map(
        functools.partial(layer, nx, mesh.shape["emb"] // nx, mesh.shape["dp"]),
        mesh=mesh,
        in_specs=(
            P("emb", None),
            P(("dp", "emb"), None),
            P(("dp", "emb")),
            P(("dp", "emb"), None),
            P(("dp", "emb"), None),
            P(),
            P(),
        ),
        out_specs=(P(("dp", "emb"), None), P(("emb", "dp"), None)),
        check_vma=False,
    )
```

time: 286 us -> 116 us (0.41)
  waiting for transfers between devices: 174 us -> 0 us
  Pallas kernels: 0 us -> 107 us
  blocking collectives: 35.9 us -> 0 us
  matrix products: 19.8 us -> 0 us
  starting transfers between devices: 15 us -> 0 us
  between operations: 14.4 us -> 0.66 us
  other arithmetic: 13.3 us -> 0 us
  local copies, waits for them, and re-layouts: 13.5 us -> 7.99 us
    psum x1 -> x0, waiting for transfers between devices: 120 us -> none  [body(): totals = lax.psum(dense.astype(jnp.bfloat16), 'dp').astype(jnp.float32)]
    pallas_call x0 -> x1, Pallas kernels: none -> 107 us  [layer(): pl.pallas_call(functools.partial(kernel, nx, nz, nd, chunks), out_shape=(...]
    all_to_all x2 -> x0, waiting for transfers between devices: 53.7 us -> none  [the longest x1 27.6 us: body(): lax.all_to_all(fetched, 'emb', split_axis=0, concat_axis=0, tiled=True)]
    all_to_all x1 -> x0, blocking collectives: 35.9 us -> none  [body(): lax.all_to_all(requests, 'emb', split_axis=0, concat_axis=0, tiled=True)]
    dot_general x11 -> x0, matrix products: 19.8 us -> none  [the longest x3 5.83 us: layer(): jnp.einsum('hqk,khd->qhd', weights, values, preferred_element_type=jnp.fl...]
    all_to_all x2 -> x0, starting transfers between devices: 14.8 us -> none  [the longest x1 9.96 us: body(): lax.all_to_all(outgoing, 'emb', split_axis=0, concat_axis=0, tiled=True)]
    unnamed x28 -> x16, local copies, waits for them, and re-layouts: 1.46 us -> 7.99 us
    scatter-add x1 -> x0, other arithmetic: 5.14 us -> none  [body(): dense = jnp.zeros((rows_here, width), jnp.float32).at[placed].add(incomin...]
  transfers between devices with their start and end apart: 3 -> 0, of which waited for: 3 -> 0; matrix products, arithmetic and copies ran while one was open for 1% -> 0% of each run, Pallas kernels for 0% -> 0%
where the time goes in v1:
time: 116 us; the launch traced here: 115 us
  Pallas kernels  107 us (92%)
  local copies, waits for them, and re-layouts  7.99 us (7%)
    pallas_call x1, Pallas kernels, layer(): pl.pallas_call(functools.partial(kernel, nx, nz, nd, chunks), out_shape=(...  107 us
    unnamed x16, local copies, waits for them, and re-layouts  7.99 us

profile of v1, /device:TPU:1, one launch (start us, length us, event | category | flops | bytes accessed | tf_op | source)
XLA Modules:
  0.0 115.4 jit_solution(16692154491948603508)
XLA Ops:
  0.6 0.0 copy-start
  0.6 1.6 %copy-done = bf16[512,2048]{1,0:T(8,128)(2,1)S(1)} copy-done((bf16[512,2048]{1,0:T(8,128)(2,1)S(1)}, bf16[512,2048]{1,0:T(8,128)(2,1)}, u32[]{:S(2)}) %copy-start) | copy-done | bytes 2097176
  2.2 0.0 copy-start.1
  2.2 1.0 copy-done.1
  3.3 0.0 copy-start.2
  3.3 1.0 copy-done.2
  4.3 0.0 copy-start.3
  4.3 0.9 copy-done.3
  5.3 0.0 copy-start.4
  5.3 0.7 copy-done.4
  5.9 0.0 copy-start.5
  5.9 0.7 copy-done.5
  6.6 0.0 copy-start.6
  6.6 0.7 copy-done.6
  7.3 106.7 %hstu.1 = (bf16[256,512]{1,0:T(8,128)(2,1)S(1)}, f32[32,512]{1,0:T(8,128)S(1)}) custom-call(s32[1,256]{1,0:T(1,128)S(1)} %bitcast.2, s32[1,256]{1,0:T(1,128)S(1)} %bitcast.3, s32[1,256]{1,0:T(1,128)S(1)} %copy-done.6, bf16[512,512]{1,0:T(8,128)(2,1)S(1)} %copy-done.1, bf16[256,512]{1,0:T(8,128)(2,1)S(1)} %copy-done.3, bf16[512,2048]{1,0:T(8,128)(2,1)S(1)} %copy-done, ...), custom_call_target="tpu_custom_call" | custom-call | tf_op jit(solution)/shard_map/hstu/pallas_call | solution.py:331
  114.0 0.7 copy.11
  114.8 0.6 copy.12
Async XLA Ops:
  0.6 1.6 %copy-start = (bf16[512,2048]{1,0:T(8,128)(2,1)S(1)}, bf16[512,2048]{1,0:T(8,128)(2,1)}, u32[]{:S(2)}) copy-start(bf16[512,2048]{1,0:T(8,128)(2,1)} %win_hbm.1) | copy-start | bytes 6291460
  2.2 1.0 copy-start.1
  3.3 1.0 copy-start.2
  4.3 0.9 copy-start.3
  5.3 0.7 copy-start.4
  5.9 0.7 copy-start.5
  6.6 0.7 copy-start.6

commit v2 on v1

--- a/solution.py
+++ b/solution.py
@@ -38,7 +38,7 @@
     return jnp.where(step % 2 == 1, (step + 1) // 2, size - step // 2)
 
 
-def forward_backward(seg_row, x_ref, grad_ref, win_ref, wout_ref, mixed_ref, dx_ref,
+def forward_backward(seg_row, x_ref, grad_ref, win_ref, wout_ref, gated_ref, dx_ref,
                      proj_ref, slope_ref, weight_ref, wslope_ref, dz_ref):
     tokens, width = x_ref.shape
     pairs = HEADS // 2
@@ -89,8 +89,7 @@
     rstd = lax.rsqrt(jnp.mean(center * center, axis=1, keepdims=True) + 1e-05)
     normed = center * rstd
     u = proj_ref[:, part(0)].astype(F32)
-    gated = (normed * u).astype(BF16)
-    mixed_ref[...] = (dot(gated, wout_ref[...]) + x.astype(F32)).astype(BF16)
+    gated_ref[...] = (normed * u).astype(BF16)
 
     d_gated = dot(grad_ref[...], wout_ref[...], (1, 1)).astype(BF16).astype(F32)
     d_u = (d_gated * normed).astype(BF16).astype(F32)
@@ -121,12 +120,12 @@
 
 
 def kernel(nx, nz, nd, chunks,
-           owner_ref, row_ref, seg_ref, table_hbm, grad_hbm, win_hbm, wout_hbm,
+           owner_hbm, row_hbm, seg_hbm, table_hbm, grad_hbm, win_hbm, wout_hbm,
            mixed_ref, out_ref,
-           table_ref, grad_ref, win_ref, wout_ref,
+           owner_ref, row_ref, seg_ref, table_ref, grad_ref, win_ref, wout_ref,
            ask_ref, mid_ref, comb_ref, fin_ref,
            place_ref, back_ref, put_ref,
-           send_ref, recv_ref, x_ref, dx_ref,
+           send_ref, recv_ref, x_ref, gated_ref, dx_ref,
            proj_ref, slope_ref, weight_ref, wslope_ref, dz_ref,
            gsend_ref, grecv_ref, dsend_ref, drecv_ref,
            load_sem, zs_sem, zr_sem, xs_sem, xr_sem, rs_sem, rr_sem, gs_sem, gr_sem, ds_sem, dr_sem):
@@ -137,12 +136,12 @@
     tokens, width = x_ref.shape
     rows = table_ref.shape[0]
     lanes = nz * CAP
-    half = width // (2 * chunks)
 
     loads = [
         pltpu.make_async_copy(source, target, load_sem.at[index])
         for index, (source, target) in enumerate(
-            [(table_hbm, table_ref), (win_hbm, win_ref), (wout_hbm, wout_ref), (grad_hbm, grad_ref)]
+            [(owner_hbm, owner_ref), (row_hbm, row_ref), (seg_hbm, seg_ref), (table_hbm, table_ref),
+             (win_hbm, win_ref), (wout_hbm, wout_ref), (grad_hbm, grad_ref)]
         )
     ]
     for load in loads:
@@ -150,20 +149,28 @@
 
     barrier = pltpu.get_barrier_semaphore()
 
-    def greet(step, carry):
-        pl.semaphore_signal(barrier, 1, device_id={"emb": (emb + step) % groups}, device_id_type=MESH)
+    def greet_z(step, carry):
+        peer = x_at * nz + (z_at + step) % nz
+        pl.semaphore_signal(barrier, 1, device_id={"emb": peer}, device_id_type=MESH)
+        return carry
+
+    def greet_x(step, carry):
+        peer = (x_at + step) % nx * nz + z_at
+        pl.semaphore_signal(barrier, 1, device_id={"emb": peer}, device_id_type=MESH)
         return carry
 
     def greet_dp(step, carry):
         pl.semaphore_signal(barrier, 1, device_id={"dp": (dp + step) % nd}, device_id_type=MESH)
         return carry
 
-    lax.fori_loop(1, groups, greet, 0)
+    lax.fori_loop(1, nz, greet_z, 0)
+    lax.fori_loop(1, nx, greet_x, 0)
     lax.fori_loop(1, nd, greet_dp, 0)
 
     def finish(ref, count, sem):
         pltpu.make_async_copy(ref.at[pl.ds(0, count)], ref.at[pl.ds(0, count)], sem).wait()
 
+    loads[0].wait()
     owner = owner_ref[...].astype(F32)
     named = iota((groups, tokens), 0).astype(F32) == owner
     before = (iota((tokens, tokens), 0) < iota((tokens, tokens), 1)).astype(BF16)
@@ -172,6 +179,7 @@
     target = owner * CAP + slot
     place_ref[...] = (to_col(target) == iota((tokens, groups * CAP), 1).astype(F32)).astype(BF16)
     back_ref[...] = (iota((groups * CAP, tokens), 0).astype(F32) == target).astype(BF16)
+    loads[1].wait()
     number = to_col((row_ref[...] + 1).astype(F32))
     lane = to_col(slot) + (z_at * CAP).astype(F32)
     here = lane == iota((tokens, lanes), 1).astype(F32)
@@ -183,7 +191,7 @@
     for at in range(nx):
         ask_ref[:, pl.ds(at, 1), :] = ask[at * nz:(at + 1) * nz].reshape(nz, 1, lanes)
 
-    pl.semaphore_wait(barrier, groups + nd - 2)
+    pl.semaphore_wait(barrier, nz + nx + nd - 3)
 
     def ask_z(step, carry):
         peer = (z_at + near(step, nz)) % nz
@@ -224,27 +232,26 @@
         lax.fori_loop(first, nz + first, send, 0) if first == 0 else lax.fori_loop(1, nz, send, 0)
 
     def blocks(value):
+        half = value.shape[1] // 2
         left = value[:, :half].reshape(nz, CAP, half)
         right = value[:, half:].reshape(nz, CAP, half)
         return jnp.concatenate([left, right], axis=1).astype(BF16)
 
     def unblocks(value):
+        half = value.shape[2]
         value = value.astype(F32)
         left = value[:, :CAP].reshape(groups * CAP, half)
         right = value[:, CAP:].reshape(groups * CAP, half)
         return jnp.concatenate([left, right], axis=1).astype(BF16)
 
-    loads[0].wait()
+    loads[3].wait()
 
     def answer(step, first):
         at = (x_at + step) % nx
         asked = to_col(fin_ref[at])
         pick = (asked == (iota((lanes, rows), 1) + 1).astype(F32)).astype(BF16)
-        for side in range(chunks):
-            cols = slice(side * 2 * half, (side + 1) * 2 * half)
-            send_ref[side, pl.ds(at * nz, nz)] = blocks(dot(pick, table_ref[:, cols]))
-        for side in range(chunks):
-            send_group(first, at, send_ref.at[side], recv_ref.at[side], rs_sem.at[side], rr_sem.at[side])
+        send_ref[pl.ds(at * nz, nz)] = blocks(dot(pick, table_ref[...]))
+        send_group(first, at, send_ref, recv_ref, rs_sem, rr_sem)
 
     answer(0, 1)
 
@@ -253,24 +260,22 @@
         return carry
 
     lax.fori_loop(1, nx, answer_other, 0)
-    for side in range(chunks):
-        recv_ref[side, emb] = send_ref[side, emb]
+    recv_ref[emb] = send_ref[emb]
 
     asked = jnp.concatenate([fin_ref[at] for at in range(nx)], axis=1)
     put_ref[...] = ((iota((rows, groups * CAP), 0) + 1).astype(F32) == asked).astype(BF16)
 
+    finish(recv_ref, groups - 1, rr_sem)
+    x_ref[...] = dot(place_ref[...], unblocks(recv_ref[...])).astype(BF16)
+
+    for index in (2, 4, 5, 6):
+        loads[index].wait()
+    forward_backward(seg_ref[...].astype(F32), x_ref, grad_ref, win_ref, wout_ref, gated_ref, dx_ref,
+                     proj_ref, slope_ref, weight_ref, wslope_ref, dz_ref)
+
+    part = width // chunks
     for side in range(chunks):
-        finish(recv_ref.at[side], groups - 1, rr_sem.at[side])
-        cols = slice(side * 2 * half, (side + 1) * 2 * half)
-        x_ref[:, cols] = dot(place_ref[...], unblocks(recv_ref[side])).astype(BF16)
-
-    for load in loads[1:]:
-        load.wait()
-    forward_backward(seg_ref[...].astype(F32), x_ref, grad_ref, win_ref, wout_ref, mixed_ref, dx_ref,
-                     proj_ref, slope_ref, weight_ref, wslope_ref, dz_ref)
-
-    for side in range(chunks):
-        cols = slice(side * 2 * half, (side + 1) * 2 * half)
+        cols = slice(side * part, (side + 1) * part)
 
         def give(step, first):
             at = (x_at + step) % nx
@@ -287,10 +292,12 @@
         lax.fori_loop(1, nx, give_other, 0)
         grecv_ref[side, emb] = gsend_ref[side, emb]
 
+    mixed_ref[...] = (dot(gated_ref[...], wout_ref[...]) + x_ref[...].astype(F32)).astype(BF16)
+
     for side in range(chunks):
         finish(grecv_ref.at[side], groups - 1, gr_sem.at[side])
         dense = dot(put_ref[...], unblocks(grecv_ref[side]))
-        dsend_ref[side] = dense.reshape(nd, rows // nd, 2 * half).astype(BF16)
+        dsend_ref[side] = dense.reshape(nd, rows // nd, part).astype(BF16)
 
         def send_dp(step, carry):
             peer = (dp + step) % nd
@@ -306,13 +313,13 @@
 
     for side in range(chunks):
         finish(drecv_ref.at[side], nd - 1, dr_sem.at[side])
-        cols = slice(side * 2 * half, (side + 1) * 2 * half)
+        cols = slice(side * part, (side + 1) * part)
         out_ref[:, cols] = jnp.sum(drecv_ref[side].astype(F32), axis=0)
 
     finish(ask_ref, nz - 1, zs_sem)
     finish(comb_ref, nx - 1, xs_sem)
+    finish(send_ref, groups - 1, rs_sem)
     for side in range(chunks):
-        finish(send_ref.at[side], groups - 1, rs_sem.at[side])
         finish(gsend_ref.at[side], groups - 1, gs_sem.at[side])
         finish(dsend_ref.at[side], nd - 1, ds_sem.at[side])
 
@@ -322,8 +329,8 @@
     rows = table.shape[0]
     groups = nx * nz
     lanes = nz * CAP
-    chunks = 1
-    half = width // (2 * chunks)
+    chunks = 2
+    part = width // chunks
     vmem = pl.BlockSpec(memory_space=pltpu.VMEM)
     anywhere = pl.BlockSpec(memory_space=pl.ANY)
     dma = pltpu.SemaphoreType.DMA
@@ -331,12 +338,15 @@
     return pl.pallas_call(
         functools.partial(kernel, nx, nz, nd, chunks),
         out_shape=(
-            jax.ShapeDtypeStruct((tokens, width), BF16),
-            jax.ShapeDtypeStruct((rows // nd, width), F32),
+            pltpu.VMEM((tokens, width), BF16),
+            pltpu.VMEM((rows // nd, width), F32),
         ),
-        in_specs=[vmem] * 3 + [anywhere] * 4,
+        in_specs=[anywhere] * 7,
         out_specs=(vmem, vmem),
         scratch_shapes=[
+            pltpu.VMEM((1, tokens), jnp.int32),
+            pltpu.VMEM((1, tokens), jnp.int32),
+            pltpu.VMEM((1, tokens), jnp.int32),
             pltpu.VMEM((rows, width), BF16),
             pltpu.VMEM((tokens, width), BF16),
             pltpu.VMEM((width, 4 * width), BF16),
@@ -348,8 +358,9 @@
             pltpu.VMEM((tokens, groups * CAP), BF16),
             pltpu.VMEM((groups * CAP, tokens), BF16),
             pltpu.VMEM((rows, groups * CAP), BF16),
-            pltpu.VMEM((chunks, groups, 2 * CAP, half), BF16),
-            pltpu.VMEM((chunks, groups, 2 * CAP, half), BF16),
+            pltpu.VMEM((groups, 2 * CAP, width // 2), BF16),
+            pltpu.VMEM((groups, 2 * CAP, width // 2), BF16),
+            pltpu.VMEM((tokens, width), BF16),
             pltpu.VMEM((tokens, width), BF16),
             pltpu.VMEM((tokens, width), BF16),
             pltpu.VMEM((tokens, 4 * width), BF16),
@@ -357,15 +368,15 @@
             pltpu.VMEM((pairs, 2 * tokens, tokens), BF16),
             pltpu.VMEM((pairs, 2 * tokens, tokens), F32),
             pltpu.VMEM((tokens, 4 * width), BF16),
-            pltpu.VMEM((chunks, groups, 2 * CAP, half), BF16),
-            pltpu.VMEM((chunks, groups, 2 * CAP, half), BF16),
-            pltpu.VMEM((chunks, nd, rows // nd, 2 * half), BF16),
-            pltpu.VMEM((chunks, nd, rows // nd, 2 * half), BF16),
-            dma((4,)), dma, dma, dma, dma,
-            dma((chunks,)), dma((chunks,)), dma((chunks,)), dma((chunks,)), dma((chunks,)), dma((chunks,)),
+            pltpu.VMEM((chunks, groups, 2 * CAP, part // 2), BF16),
+            pltpu.VMEM((chunks, groups, 2 * CAP, part // 2), BF16),
+            pltpu.VMEM((chunks, nd, rows // nd, part), BF16),
+            pltpu.VMEM((chunks, nd, rows // nd, part), BF16),
+            dma((7,)), dma, dma, dma, dma,
+            dma, dma, dma((chunks,)), dma((chunks,)), dma((chunks,)), dma((chunks,)),
         ],
         compiler_params=pltpu.CompilerParams(
-            collective_id=0, has_side_effects=True, vmem_limit_bytes=48 * 2**20
+            collective_id=0, has_side_effects=True, vmem_limit_bytes=60 * 2**20
         ),
         name="hstu",
     )(item_shard.reshape(1, tokens), item_row.reshape(1, tokens), segment_ids, table, grad_out, w_in, w_out)

time: 116 us -> 101 us (0.87)
  Pallas kernels: 107 us -> 97.9 us
  local copies, waits for them, and re-layouts: 7.99 us -> 1.33 us
    pallas_call x1, Pallas kernels: 107 us -> 97.9 us  [layer(): pl.pallas_call(functools.partial(kernel, nx, nz, nd, chunks), out_shape=(...]
    unnamed x16 -> x2, local copies, waits for them, and re-layouts: 7.99 us -> 1.33 us
where the time goes in v2:
time: 101 us; the launch traced here: 99.9 us
  Pallas kernels  97.9 us (97%)
  local copies, waits for them, and re-layouts  1.33 us (1%)
    pallas_call x1, Pallas kernels, layer(): pl.pallas_call(functools.partial(kernel, nx, nz, nd, chunks), out_shape=(...  97.9 us

profile of v2, /device:TPU:1, one launch (start us, length us, event | category | flops | bytes accessed | tf_op | source)
XLA Modules:
  0.0 99.9 jit_solution(5906722255871755321)
XLA Ops:
  0.6 97.9 %hstu.1 = (bf16[256,512]{1,0:T(8,128)(2,1)S(1)}, f32[32,512]{1,0:T(8,128)S(1)}) custom-call(s32[1,256]{1,0:T(1,128)} %bitcast.2, s32[1,256]{1,0:T(1,128)} %bitcast.3, s32[1,256]{1,0:T(1,128)} %seg_hbm.1, bf16[512,512]{1,0:T(8,128)(2,1)} %table_hbm.1, bf16[256,512]{1,0:T(8,128)(2,1)} %grad_hbm.1, bf16[512,2048]{1,0:T(8,128)(2,1)} %win_hbm.1, ...), custom_call_target="tpu_custom_call" | custom-call | tf_op jit(solution)/shard_map/hstu/pallas_call | solution.py:338
  98.6 0.7 copy.11
  99.3 0.6 copy.12

commit v3 on v2

--- a/solution.py
+++ b/solution.py
@@ -34,8 +34,21 @@
     return 0.5 * jnp.tanh(0.5 * value) + 0.5
 
 
-def near(step, size):
-    return jnp.where(step % 2 == 1, (step + 1) // 2, size - step // 2)
+def ahead(at, distance, size):
+    to = at + distance
+    return jnp.where(to >= size, to - size, to)
+
+
+def around(at, size, act):
+    act(ahead(at, size // 2, size))
+
+    def both(step, carry):
+        distance = size // 2 - 1 - step
+        act(ahead(at, distance, size))
+        act(ahead(at, size - distance, size))
+        return carry
+
+    lax.fori_loop(0, size // 2 - 1, both, 0)
 
 
 def forward_backward(seg_row, x_ref, grad_ref, win_ref, wout_ref, gated_ref, dx_ref,
@@ -119,16 +132,17 @@
     dx_ref[...] = (d_x + grad_ref[...].astype(F32)).astype(BF16)
 
 
-def kernel(nx, nz, nd, chunks,
+def kernel(nx, nz, nd,
            owner_hbm, row_hbm, seg_hbm, table_hbm, grad_hbm, win_hbm, wout_hbm,
            mixed_ref, out_ref,
            owner_ref, row_ref, seg_ref, table_ref, grad_ref, win_ref, wout_ref,
-           ask_ref, mid_ref, comb_ref, fin_ref,
-           place_ref, back_ref, put_ref,
+           ask_ref, mid_ref, comb_ref, fin_ref, pask_ref, pmid_ref, pcomb_ref, pfin_ref,
+           place_ref, back_ref, pback_ref, put_ref, pput_ref,
            send_ref, recv_ref, x_ref, gated_ref, dx_ref,
            proj_ref, slope_ref, weight_ref, wslope_ref, dz_ref,
-           gsend_ref, grecv_ref, dsend_ref, drecv_ref,
-           load_sem, zs_sem, zr_sem, xs_sem, xr_sem, rs_sem, rr_sem, gs_sem, gr_sem, ds_sem, dr_sem):
+           gsend_ref, grecv_ref, psend_ref, precv_ref, dsend_ref, drecv_ref, bsend_ref, brecv_ref,
+           load_sem, zs_sem, zr_sem, xs_sem, xr_sem, ps_sem, pr_sem, qs_sem, qr_sem, rs_sem, rr_sem,
+           gs_sem, gr_sem, hs_sem, hr_sem, ds_sem, dr_sem, bs_sem, br_sem):
     emb = lax.axis_index("emb")
     dp = lax.axis_index("dp")
     x_at, z_at = emb // nz, emb % nz
@@ -136,6 +150,26 @@
     tokens, width = x_ref.shape
     rows = table_ref.shape[0]
     lanes = nz * CAP
+
+    barrier = pltpu.get_barrier_semaphore()
+
+    def greet(peer, axis):
+        pl.semaphore_signal(barrier, 1, device_id={axis: peer}, device_id_type=MESH)
+
+    ny = nd // 2
+    far = [way for step in range(ny // 2, 0, -1) for way in ((step, ny - step) if 2 * step < ny else (step,))]
+    y_at, core_at = dp // 2, dp % 2
+    k_at = y_at + ny * core_at
+    plane = [(ahead(y_at, way, ny), core) for way in far for core in range(2)] + [(y_at, 1 - core_at)]
+    plane = [(y * 2 + core, y + ny * core) for y, core in plane]
+    dp_peers = [peer for peer, _ in plane]
+    x_all = [ahead(x_at, step, nx) for step in range(nx)]
+
+    around(z_at, nz, lambda to: greet(x_at * nz + to, "emb"))
+    for to in x_all[1:]:
+        greet(to * nz + z_at, "emb")
+    for peer in dp_peers:
+        greet(peer, "dp")
 
     loads = [
         pltpu.make_async_copy(source, target, load_sem.at[index])
@@ -147,26 +181,6 @@
     for load in loads:
         load.start()
 
-    barrier = pltpu.get_barrier_semaphore()
-
-    def greet_z(step, carry):
-        peer = x_at * nz + (z_at + step) % nz
-        pl.semaphore_signal(barrier, 1, device_id={"emb": peer}, device_id_type=MESH)
-        return carry
-
-    def greet_x(step, carry):
-        peer = (x_at + step) % nx * nz + z_at
-        pl.semaphore_signal(barrier, 1, device_id={"emb": peer}, device_id_type=MESH)
-        return carry
-
-    def greet_dp(step, carry):
-        pl.semaphore_signal(barrier, 1, device_id={"dp": (dp + step) % nd}, device_id_type=MESH)
-        return carry
-
-    lax.fori_loop(1, nz, greet_z, 0)
-    lax.fori_loop(1, nx, greet_x, 0)
-    lax.fori_loop(1, nd, greet_dp, 0)
-
     def finish(ref, count, sem):
         pltpu.make_async_copy(ref.at[pl.ds(0, count)], ref.at[pl.ds(0, count)], sem).wait()
 
@@ -177,65 +191,98 @@
     named_bf = named.astype(BF16)
     slot = jnp.sum(jnp.where(named, dot(named_bf, before), 0.0), axis=0, keepdims=True)
     target = owner * CAP + slot
-    place_ref[...] = (to_col(target) == iota((tokens, groups * CAP), 1).astype(F32)).astype(BF16)
-    back_ref[...] = (iota((groups * CAP, tokens), 0).astype(F32) == target).astype(BF16)
     loads[1].wait()
     number = to_col((row_ref[...] + 1).astype(F32))
-    lane = to_col(slot) + (z_at * CAP).astype(F32)
-    here = lane == iota((tokens, lanes), 1).astype(F32)
+    slot_col = to_col(slot)
+    lane_at = iota((tokens, lanes), 1).astype(F32)
+    here = slot_col + (z_at * CAP).astype(F32) == lane_at
     high = jnp.floor(number * (1.0 / 16.0))
     low = number - 16.0 * high
-    ask = 16.0 * dot(named_bf, jnp.where(here, high, 0.0).astype(BF16)) + dot(
-        named_bf, jnp.where(here, low, 0.0).astype(BF16)
-    )
+
+    def numbers(named_bf, here):
+        return 16.0 * dot(named_bf, jnp.where(here, high, 0.0).astype(BF16)) + dot(
+            named_bf, jnp.where(here, low, 0.0).astype(BF16)
+        )
+
+    ask = numbers(named_bf, here)
     for at in range(nx):
         ask_ref[:, pl.ds(at, 1), :] = ask[at * nz:(at + 1) * nz].reshape(nz, 1, lanes)
 
     pl.semaphore_wait(barrier, nz + nx + nd - 3)
 
-    def ask_z(step, carry):
-        peer = (z_at + near(step, nz)) % nz
+    def ask_z(peer):
         pltpu.make_async_remote_copy(
             src_ref=ask_ref.at[peer], dst_ref=mid_ref.at[z_at], send_sem=zs_sem, recv_sem=zr_sem,
             device_id={"emb": x_at * nz + peer}, device_id_type=MESH,
         ).start()
-        return carry
-
-    lax.fori_loop(1, nz, ask_z, 0)
+
+    around(z_at, nz, ask_z)
     mid_ref[z_at] = ask_ref[z_at]
+
+    owner_x = jnp.floor(owner * (1.0 / nz))
+    ahead_z = owner - nz * owner_x - z_at.astype(F32)
+    ahead_z = jnp.where(ahead_z < 0.0, ahead_z + nz, ahead_z)
+    behind_z = jnp.where(ahead_z > 0.0, nz - ahead_z, 0.0)
+    served = [owner_x * nz + ahead_z, owner_x * nz + behind_z]
+    here = slot_col + (dp * CAP).astype(F32) == lane_at
+    device = iota((groups, tokens), 0).astype(F32)
+    pask = numbers(jnp.concatenate([device == one for one in served], axis=0).astype(BF16), here)
+    for at in range(2 * nx):
+        pask_ref[:, pl.ds(at, 1), :] = pask[at % 2 * groups + at // 2 * nz:][:nz].reshape(nz, 1, lanes)
+    for peer, k in plane:
+        pltpu.make_async_remote_copy(
+            src_ref=pask_ref.at[k], dst_ref=pmid_ref.at[dp], send_sem=ps_sem, recv_sem=pr_sem,
+            device_id={"dp": peer}, device_id_type=MESH,
+        ).start()
+    pmid_ref[dp] = pask_ref[k_at]
+
     finish(mid_ref, nz - 1, zr_sem)
     comb = jnp.sum(mid_ref[...], axis=0)
     for at in range(nx):
         comb_ref[at] = comb[at:at + 1]
 
-    def ask_x(step, carry):
-        peer = (x_at + step) % nx
+    for peer in x_all[1:]:
         pltpu.make_async_remote_copy(
             src_ref=comb_ref.at[peer], dst_ref=fin_ref.at[x_at], send_sem=xs_sem, recv_sem=xr_sem,
             device_id={"emb": peer * nz + z_at}, device_id_type=MESH,
         ).start()
-        return carry
-
-    lax.fori_loop(1, nx, ask_x, 0)
     fin_ref[x_at] = comb_ref[x_at]
-    finish(fin_ref, nx - 1, xr_sem)
-
-    def send_group(first, at, source, target, send_sem, recv_sem):
-        def send(step, carry):
-            peer = at * nz + (z_at + near(step, nz)) % nz
+
+    finish(pmid_ref, nd - 1, pr_sem)
+    pcomb = jnp.sum(pmid_ref[...], axis=0)
+    for at in range(nx):
+        pcomb_ref[at] = pcomb[2 * at:2 * at + 2]
+    for peer in x_all[1:]:
+        pltpu.make_async_remote_copy(
+            src_ref=pcomb_ref.at[peer], dst_ref=pfin_ref.at[x_at], send_sem=qs_sem, recv_sem=qr_sem,
+            device_id={"emb": peer * nz + z_at}, device_id_type=MESH,
+        ).start()
+    pfin_ref[x_at] = pcomb_ref[x_at]
+
+    def send_all(places, source, target, send_sem, recv_sem):
+        def send(peer):
             pltpu.make_async_remote_copy(
                 src_ref=source.at[peer], dst_ref=target.at[emb], send_sem=send_sem, recv_sem=recv_sem,
                 device_id={"emb": peer}, device_id_type=MESH,
             ).start()
-            return carry
-
-        lax.fori_loop(first, nz + first, send, 0) if first == 0 else lax.fori_loop(1, nz, send, 0)
+
+        def send_z(to):
+            for at in places:
+                send(at * nz + to)
+
+        around(z_at, nz, send_z)
+        for at in places:
+            if at is not x_all[0]:
+                send(at * nz + z_at)
 
     def blocks(value):
         half = value.shape[1] // 2
         left = value[:, :half].reshape(nz, CAP, half)
         right = value[:, half:].reshape(nz, CAP, half)
         return jnp.concatenate([left, right], axis=1).astype(BF16)
+
+    def together(value):
+        return jnp.concatenate([blocks(value[at * lanes:(at + 1) * lanes]) for at in range(nx)], axis=0)
 
     def unblocks(value):
         half = value.shape[2]
@@ -246,24 +293,30 @@
 
     loads[3].wait()
 
-    def answer(step, first):
-        at = (x_at + step) % nx
+    def answer(at):
         asked = to_col(fin_ref[at])
         pick = (asked == (iota((lanes, rows), 1) + 1).astype(F32)).astype(BF16)
         send_ref[pl.ds(at * nz, nz)] = blocks(dot(pick, table_ref[...]))
-        send_group(first, at, send_ref, recv_ref, rs_sem, rr_sem)
-
-    answer(0, 1)
-
-    def answer_other(step, carry):
-        answer(step, 0)
-        return carry
-
-    lax.fori_loop(1, nx, answer_other, 0)
+
+    answer(x_at)
+    send_all(x_all[:1], send_ref, recv_ref, rs_sem, rr_sem)
+    finish(fin_ref, nx - 1, xr_sem)
+    for at in x_all[1:]:
+        answer(at)
+    send_all(x_all[1:], send_ref, recv_ref, rs_sem, rr_sem)
     recv_ref[emb] = send_ref[emb]
 
-    asked = jnp.concatenate([fin_ref[at] for at in range(nx)], axis=1)
-    put_ref[...] = ((iota((rows, groups * CAP), 0) + 1).astype(F32) == asked).astype(BF16)
+    place_ref[...] = (to_col(target) == iota((tokens, groups * CAP), 1).astype(F32)).astype(BF16)
+    at_slot = iota((groups * CAP, tokens), 0).astype(F32)
+    back_ref[...] = (at_slot == target).astype(BF16)
+    for which in range(2):
+        pback_ref[which] = (at_slot == served[which] * CAP + slot).astype(BF16)
+    at_row = (iota((rows, groups * CAP), 0) + 1).astype(F32)
+    put_ref[...] = (at_row == jnp.concatenate([fin_ref[at] for at in range(nx)], axis=1)).astype(BF16)
+    finish(pfin_ref, nx - 1, qr_sem)
+    for which in range(2):
+        asked = jnp.concatenate([pfin_ref[at][which:which + 1] for at in range(nx)], axis=1)
+        pput_ref[which] = (at_row == asked).astype(BF16)
 
     finish(recv_ref, groups - 1, rr_sem)
     x_ref[...] = dot(place_ref[...], unblocks(recv_ref[...])).astype(BF16)
@@ -273,55 +326,89 @@
     forward_backward(seg_ref[...].astype(F32), x_ref, grad_ref, win_ref, wout_ref, gated_ref, dx_ref,
                      proj_ref, slope_ref, weight_ref, wslope_ref, dz_ref)
 
-    part = width // chunks
-    for side in range(chunks):
-        cols = slice(side * part, (side + 1) * part)
-
-        def give(step, first):
-            at = (x_at + step) % nx
-            mine = back_ref[pl.ds(pl.multiple_of(at * lanes, lanes), lanes), :]
-            gsend_ref[side, pl.ds(at * nz, nz)] = blocks(dot(mine, dx_ref[:, cols]))
-            send_group(first, at, gsend_ref.at[side], grecv_ref.at[side], gs_sem.at[side], gr_sem.at[side])
-
-        give(0, 1)
-
-        def give_other(step, carry):
-            give(step, 0)
-            return carry
-
-        lax.fori_loop(1, nx, give_other, 0)
-        grecv_ref[side, emb] = gsend_ref[side, emb]
+    part = width // 2
+    quarter = part // 2
+    gsend_ref[...] = together(dot(back_ref[...], dx_ref[:, :part]))
+    send_all(x_all, gsend_ref, grecv_ref, gs_sem, gr_sem)
+    grecv_ref[emb] = gsend_ref[emb]
+
+    given = [dot(pback_ref[which], dx_ref[:, part + which * quarter:][:, :quarter]) for which in range(2)]
+    psend_ref[...] = together(jnp.concatenate(given, axis=1))
+    for peer, k in plane + [(dp, k_at)]:
+        for at in x_all:
+            if peer is dp and at is x_all[0]:
+                continue
+            pltpu.make_async_remote_copy(
+                src_ref=psend_ref.at[at * nz + k], dst_ref=precv_ref.at[x_at * nd + dp],
+                send_sem=hs_sem, recv_sem=hr_sem,
+                device_id={"dp": peer, "emb": at * nz + z_at}, device_id_type=MESH,
+            ).start()
+    precv_ref[x_at * nd + dp] = psend_ref[x_at * nz + k_at]
 
     mixed_ref[...] = (dot(gated_ref[...], wout_ref[...]) + x_ref[...].astype(F32)).astype(BF16)
 
-    for side in range(chunks):
-        finish(grecv_ref.at[side], groups - 1, gr_sem.at[side])
-        dense = dot(put_ref[...], unblocks(grecv_ref[side]))
-        dsend_ref[side] = dense.reshape(nd, rows // nd, part).astype(BF16)
-
-        def send_dp(step, carry):
-            peer = (dp + step) % nd
-            pltpu.make_async_remote_copy(
-                src_ref=dsend_ref.at[side, peer], dst_ref=drecv_ref.at[side, dp],
-                send_sem=ds_sem.at[side], recv_sem=dr_sem.at[side],
-                device_id={"dp": peer}, device_id_type=MESH,
+    finish(precv_ref, groups - 1, hr_sem)
+    taken = unblocks(precv_ref[...])
+    for which in range(2):
+        dense = dot(pput_ref[which], taken[:, which * quarter:(which + 1) * quarter])
+        bsend_ref[which] = dense.reshape(nd, rows // nd, quarter).astype(BF16)
+    homes = [x_at * nz + ahead(z_at, k_at, nz), x_at * nz + ahead(z_at, jnp.where(k_at > 0, nz - k_at, 0), nz)]
+
+    def home(which, peer):
+        return pltpu.make_async_remote_copy(
+            src_ref=bsend_ref.at[which, peer], dst_ref=brecv_ref.at[which, z_at],
+            send_sem=bs_sem.at[which], recv_sem=br_sem.at[which],
+            device_id={"dp": peer, "emb": homes[which]}, device_id_type=MESH,
+        )
+
+    for peer in dp_peers:
+        for which in range(2):
+            home(which, peer).start()
+
+    @pl.when(k_at > 0)
+    def _():
+        for which in range(2):
+            home(which, dp).start()
+
+    @pl.when(k_at == 0)
+    def _():
+        for which in range(2):
+            pltpu.make_async_copy(
+                bsend_ref.at[which, dp], brecv_ref.at[which, z_at], br_sem.at[which]
             ).start()
-            return carry
-
-        lax.fori_loop(1, nd, send_dp, 0)
-        drecv_ref[side, dp] = dsend_ref[side, dp]
-
-    for side in range(chunks):
-        finish(drecv_ref.at[side], nd - 1, dr_sem.at[side])
-        cols = slice(side * part, (side + 1) * part)
-        out_ref[:, cols] = jnp.sum(drecv_ref[side].astype(F32), axis=0)
+
+    finish(grecv_ref, groups - 1, gr_sem)
+    dense = dot(put_ref[...], unblocks(grecv_ref[...]))
+    dsend_ref[...] = dense.reshape(nd, rows // nd, part).astype(BF16)
+    for peer in dp_peers:
+        pltpu.make_async_remote_copy(
+            src_ref=dsend_ref.at[peer], dst_ref=drecv_ref.at[dp], send_sem=ds_sem, recv_sem=dr_sem,
+            device_id={"dp": peer}, device_id_type=MESH,
+        ).start()
+    drecv_ref[dp] = dsend_ref[dp]
+
+    finish(drecv_ref, nd - 1, dr_sem)
+    out_ref[:, :part] = jnp.sum(drecv_ref[...].astype(F32), axis=0)
+    for which in range(2):
+        finish(brecv_ref.at[which], nz, br_sem.at[which])
+        cols = slice(part + which * quarter, part + (which + 1) * quarter)
+        out_ref[:, cols] = jnp.sum(brecv_ref[which].astype(F32), axis=0)
 
     finish(ask_ref, nz - 1, zs_sem)
     finish(comb_ref, nx - 1, xs_sem)
+    finish(pask_ref, nd - 1, ps_sem)
+    finish(pcomb_ref, nx - 1, qs_sem)
     finish(send_ref, groups - 1, rs_sem)
-    for side in range(chunks):
-        finish(gsend_ref.at[side], groups - 1, gs_sem.at[side])
-        finish(dsend_ref.at[side], nd - 1, ds_sem.at[side])
+    finish(gsend_ref, groups - 1, gs_sem)
+    finish(psend_ref, groups - 1, hs_sem)
+    finish(dsend_ref, nd - 1, ds_sem)
+    for which in range(2):
+        finish(bsend_ref.at[which], nd - 1, bs_sem.at[which])
+
+    @pl.when(k_at > 0)
+    def _():
+        for which in range(2):
+            finish(bsend_ref.at[which], 1, bs_sem.at[which])
 
 
 def layer(nx, nz, nd, table, item_shard, item_row, segment_ids, grad_out, w_in, w_out):
@@ -329,14 +416,14 @@
     rows = table.shape[0]
     groups = nx * nz
     lanes = nz * CAP
-    chunks = 2
-    part = width // chunks
+    part = width // 2
+    quarter = part // 2
     vmem = pl.BlockSpec(memory_space=pltpu.VMEM)
     anywhere = pl.BlockSpec(memory_space=pl.ANY)
     dma = pltpu.SemaphoreType.DMA
     pairs = HEADS // 2
     return pl.pallas_call(
-        functools.partial(kernel, nx, nz, nd, chunks),
+        functools.partial(kernel, nx, nz, nd),
         out_shape=(
             pltpu.VMEM((tokens, width), BF16),
             pltpu.VMEM((rows // nd, width), F32),
@@ -355,9 +442,15 @@
             pltpu.VMEM((nz, nx, lanes), F32),
             pltpu.VMEM((nx, 1, lanes), F32),
             pltpu.VMEM((nx, 1, lanes), F32),
+            pltpu.VMEM((nz, 2 * nx, lanes), F32),
+            pltpu.VMEM((nd, 2 * nx, lanes), F32),
+            pltpu.VMEM((nx, 2, lanes), F32),
+            pltpu.VMEM((nx, 2, lanes), F32),
             pltpu.VMEM((tokens, groups * CAP), BF16),
             pltpu.VMEM((groups * CAP, tokens), BF16),
+            pltpu.VMEM((2, groups * CAP, tokens), BF16),
             pltpu.VMEM((rows, groups * CAP), BF16),
+            pltpu.VMEM((2, rows, groups * CAP), BF16),
             pltpu.VMEM((groups, 2 * CAP, width // 2), BF16),
             pltpu.VMEM((groups, 2 * CAP, width // 2), BF16),
             pltpu.VMEM((tokens, width), BF16),
@@ -368,13 +461,18 @@
             pltpu.VMEM((pairs, 2 * tokens, tokens), BF16),
             pltpu.VMEM((pairs, 2 * tokens, tokens), F32),
             pltpu.VMEM((tokens, 4 * width), BF16),
-            pltpu.VMEM((chunks, groups, 2 * CAP, part // 2), BF16),
-            pltpu.VMEM((chunks, groups, 2 * CAP, part // 2), BF16),
-            pltpu.VMEM((chunks, nd, rows // nd, part), BF16),
-            pltpu.VMEM((chunks, nd, rows // nd, part), BF16),
-            dma((7,)), dma, dma, dma, dma,
-            dma, dma, dma((chunks,)), dma((chunks,)), dma((chunks,)), dma((chunks,)),
-        ],
+            pltpu.VMEM((groups, 2 * CAP, quarter), BF16),
+            pltpu.VMEM((groups, 2 * CAP, quarter), BF16),
+            pltpu.VMEM((groups, 2 * CAP, quarter), BF16),
+            pltpu.VMEM((groups, 2 * CAP, quarter), BF16),
+            pltpu.VMEM((nd, rows // nd, part), BF16),
+            pltpu.VMEM((nd, rows // nd, part), BF16),
+            pltpu.VMEM((2, nd, rows // nd, quarter), BF16),
+            pltpu.VMEM((2, nz, rows // nd, quarter), BF16),
+            dma((7,)),
+        ]
+        + [dma] * 16
+        + [dma((2,))] * 2,
         compiler_params=pltpu.CompilerParams(
             collective_id=0, has_side_effects=True, vmem_limit_bytes=60 * 2**20
         ),

time: 101 us -> 93.3 us (0.924)
  Pallas kernels: 97.9 us -> 91.2 us
    pallas_call x1, Pallas kernels: 97.9 us -> 91.2 us  [layer(): pl.pallas_call(functools.partial(kernel, nx, nz, nd), out_shape=(pltpu.VM...]
where the time goes in v3:
time: 93.3 us; the launch traced here: 93.1 us
  Pallas kernels  91.2 us (98%)
  local copies, waits for them, and re-layouts  1.33 us (1%)
    pallas_call x1, Pallas kernels, layer(): pl.pallas_call(functools.partial(kernel, nx, nz, nd), out_shape=(pltpu.VM...  91.2 us

profile of v3, /device:TPU:1, one launch (start us, length us, event | category | flops | bytes accessed | tf_op | source)
XLA Modules:
  0.0 93.1 jit_solution(3116583419725901937)
XLA Ops:
  0.6 91.2 %hstu.1 = (bf16[256,512]{1,0:T(8,128)(2,1)S(1)}, f32[32,512]{1,0:T(8,128)S(1)}) custom-call(s32[1,256]{1,0:T(1,128)} %bitcast.2, s32[1,256]{1,0:T(1,128)} %bitcast.3, s32[1,256]{1,0:T(1,128)} %seg_hbm.1, bf16[512,512]{1,0:T(8,128)(2,1)} %table_hbm.1, bf16[256,512]{1,0:T(8,128)(2,1)} %grad_hbm.1, bf16[512,2048]{1,0:T(8,128)(2,1)} %win_hbm.1, ...), custom_call_target="tpu_custom_call" | custom-call | tf_op jit(solution)/shard_map/hstu/pallas_call | solution.py:425
  91.8 0.7 copy.11
  92.5 0.6 copy.12

commit v4 on v3

--- a/solution.py
+++ b/solution.py
@@ -51,7 +51,7 @@
     lax.fori_loop(0, size // 2 - 1, both, 0)
 
 
-def forward_backward(seg_row, x_ref, grad_ref, win_ref, wout_ref, gated_ref, dx_ref,
+def forward_backward(factor_ref, d_gated_ref, x_ref, win_ref, gated_ref,
                      proj_ref, slope_ref, weight_ref, wslope_ref, dz_ref):
     tokens, width = x_ref.shape
     pairs = HEADS // 2
@@ -69,9 +69,7 @@
         proj_ref[:, part(index)] = act.astype(BF16)
         slope_ref[:, part(index)] = sig + act * (1.0 - sig)
 
-    seg_col = to_col(seg_row)
-    seen = (iota((tokens, tokens), 1) <= iota((tokens, tokens), 0)) & (seg_col == seg_row)
-    factor = jnp.where(seen, 1.0 / MOST, 0.0)
+    factor = factor_ref[...]
     factor = jnp.concatenate([factor, factor], axis=0)
     first = iota((tokens, lanes), 1) < lanes // 2
 
@@ -104,7 +102,7 @@
     u = proj_ref[:, part(0)].astype(F32)
     gated_ref[...] = (normed * u).astype(BF16)
 
-    d_gated = dot(grad_ref[...], wout_ref[...], (1, 1)).astype(BF16).astype(F32)
+    d_gated = d_gated_ref[...].astype(F32)
     d_u = (d_gated * normed).astype(BF16).astype(F32)
     dz_ref[:, part(0)] = (d_u * slope_ref[:, part(0)]).astype(BF16)
     d_normed = d_gated * u
@@ -128,9 +126,6 @@
         put(index, 2, unstack(dot(d_s, proj_ref[:, pair(index, 3)])))
         put(index, 3, dot(d_s, q, (0, 0)))
 
-    d_x = dot(dz_ref[...], win_ref[...], (1, 1)).astype(BF16).astype(F32)
-    dx_ref[...] = (d_x + grad_ref[...].astype(F32)).astype(BF16)
-
 
 def kernel(nx, nz, nd,
            owner_hbm, row_hbm, seg_hbm, table_hbm, grad_hbm, win_hbm, wout_hbm,
@@ -138,7 +133,7 @@
            owner_ref, row_ref, seg_ref, table_ref, grad_ref, win_ref, wout_ref,
            ask_ref, mid_ref, comb_ref, fin_ref, pask_ref, pmid_ref, pcomb_ref, pfin_ref,
            place_ref, back_ref, pback_ref, put_ref, pput_ref,
-           send_ref, recv_ref, x_ref, gated_ref, dx_ref,
+           send_ref, recv_ref, x_ref, gated_ref, factor_ref, d_gated_ref, wint_ref,
            proj_ref, slope_ref, weight_ref, wslope_ref, dz_ref,
            gsend_ref, grecv_ref, psend_ref, precv_ref, dsend_ref, drecv_ref, bsend_ref, brecv_ref,
            load_sem, zs_sem, zr_sem, xs_sem, xr_sem, ps_sem, pr_sem, qs_sem, qr_sem, rs_sem, rr_sem,
@@ -151,6 +146,16 @@
     rows = table_ref.shape[0]
     lanes = nz * CAP
 
+    loads = [
+        pltpu.make_async_copy(source, target, load_sem.at[index])
+        for index, (source, target) in enumerate(
+            [(owner_hbm, owner_ref), (row_hbm, row_ref), (seg_hbm, seg_ref), (table_hbm, table_ref),
+             (win_hbm, win_ref), (wout_hbm, wout_ref), (grad_hbm, grad_ref)]
+        )
+    ]
+    for load in loads[:2]:
+        load.start()
+
     barrier = pltpu.get_barrier_semaphore()
 
     def greet(peer, axis):
@@ -170,15 +175,7 @@
         greet(to * nz + z_at, "emb")
     for peer in dp_peers:
         greet(peer, "dp")
-
-    loads = [
-        pltpu.make_async_copy(source, target, load_sem.at[index])
-        for index, (source, target) in enumerate(
-            [(owner_hbm, owner_ref), (row_hbm, row_ref), (seg_hbm, seg_ref), (table_hbm, table_ref),
-             (win_hbm, win_ref), (wout_hbm, wout_ref), (grad_hbm, grad_ref)]
-        )
-    ]
-    for load in loads:
+    for load in loads[2:]:
         load.start()
 
     def finish(ref, count, sem):
@@ -218,6 +215,65 @@
 
     around(z_at, nz, ask_z)
     mid_ref[z_at] = ask_ref[z_at]
+
+    finish(mid_ref, nz - 1, zr_sem)
+    comb = jnp.sum(mid_ref[...], axis=0)
+    for at in range(nx):
+        comb_ref[at] = comb[at:at + 1]
+
+    for peer in x_all[1:]:
+        pltpu.make_async_remote_copy(
+            src_ref=comb_ref.at[peer], dst_ref=fin_ref.at[x_at], send_sem=xs_sem, recv_sem=xr_sem,
+            device_id={"emb": peer * nz + z_at}, device_id_type=MESH,
+        ).start()
+    fin_ref[x_at] = comb_ref[x_at]
+
+    def send_all(places, source, target, send_sem, recv_sem):
+        def send(peer):
+            pltpu.make_async_remote_copy(
+                src_ref=source.at[peer], dst_ref=target.at[emb], send_sem=send_sem, recv_sem=recv_sem,
+                device_id={"emb": peer}, device_id_type=MESH,
+            ).start()
+
+        def send_z(to):
+            for at in places:
+                send(at * nz + to)
+
+        around(z_at, nz, send_z)
+        for at in places:
+            if at is not x_all[0]:
+                send(at * nz + z_at)
+
+    def blocks(value):
+        half = value.shape[1] // 2
+        left = value[:, :half].reshape(nz, CAP, half)
+        right = value[:, half:].reshape(nz, CAP, half)
+        return jnp.concatenate([left, right], axis=1).astype(BF16)
+
+    def together(value):
+        return jnp.concatenate([blocks(value[at * lanes:(at + 1) * lanes]) for at in range(nx)], axis=0)
+
+    def unblocks(value):
+        half = value.shape[2]
+        value = value.astype(F32)
+        left = value[:, :CAP].reshape(groups * CAP, half)
+        right = value[:, CAP:].reshape(groups * CAP, half)
+        return jnp.concatenate([left, right], axis=1).astype(BF16)
+
+    loads[3].wait()
+
+    def answer(at):
+        asked = to_col(fin_ref[at])
+        pick = (asked == (iota((lanes, rows), 1) + 1).astype(F32)).astype(BF16)
+        send_ref[pl.ds(at * nz, nz)] = blocks(dot(pick, table_ref[...]))
+
+    answer(x_at)
+    send_all(x_all[:1], send_ref, recv_ref, rs_sem, rr_sem)
+    finish(fin_ref, nx - 1, xr_sem)
+    for at in x_all[1:]:
+        answer(at)
+    send_all(x_all[1:], send_ref, recv_ref, rs_sem, rr_sem)
+    recv_ref[emb] = send_ref[emb]
 
     owner_x = jnp.floor(owner * (1.0 / nz))
     ahead_z = owner - nz * owner_x - z_at.astype(F32)
@@ -236,17 +292,26 @@
         ).start()
     pmid_ref[dp] = pask_ref[k_at]
 
-    finish(mid_ref, nz - 1, zr_sem)
-    comb = jnp.sum(mid_ref[...], axis=0)
-    for at in range(nx):
-        comb_ref[at] = comb[at:at + 1]
-
-    for peer in x_all[1:]:
-        pltpu.make_async_remote_copy(
-            src_ref=comb_ref.at[peer], dst_ref=fin_ref.at[x_at], send_sem=xs_sem, recv_sem=xr_sem,
-            device_id={"emb": peer * nz + z_at}, device_id_type=MESH,
-        ).start()
-    fin_ref[x_at] = comb_ref[x_at]
+    place_ref[...] = (to_col(target) == iota((tokens, groups * CAP), 1).astype(F32)).astype(BF16)
+    at_slot = iota((groups * CAP, tokens), 0).astype(F32)
+    back_ref[...] = (at_slot == target).astype(BF16)
+    for which in range(2):
+        pback_ref[which] = (at_slot == served[which] * CAP + slot).astype(BF16)
+    at_row = (iota((rows, groups * CAP), 0) + 1).astype(F32)
+    put_ref[...] = (at_row == jnp.concatenate([fin_ref[at] for at in range(nx)], axis=1)).astype(BF16)
+    for index in (2, 4, 5, 6):
+        loads[index].wait()
+    seg_row = seg_ref[...].astype(F32)
+    seen = (iota((tokens, tokens), 1) <= iota((tokens, tokens), 0)) & (to_col(seg_row) == seg_row)
+    factor_ref[...] = jnp.where(seen, 1.0 / MOST, 0.0)
+    wint_ref[...] = win_ref[...].T
+    d_gated_ref[...] = dot(grad_ref[...], wout_ref[...], (1, 1)).astype(BF16)
+
+    finish(recv_ref, groups - 1, rr_sem)
+    x_ref[...] = dot(place_ref[...], unblocks(recv_ref[...])).astype(BF16)
+
+    forward_backward(factor_ref, d_gated_ref, x_ref, win_ref, gated_ref,
+                     proj_ref, slope_ref, weight_ref, wslope_ref, dz_ref)
 
     finish(pmid_ref, nd - 1, pr_sem)
     pcomb = jnp.sum(pmid_ref[...], axis=0)
@@ -259,80 +324,19 @@
         ).start()
     pfin_ref[x_at] = pcomb_ref[x_at]
 
-    def send_all(places, source, target, send_sem, recv_sem):
-        def send(peer):
-            pltpu.make_async_remote_copy(
-                src_ref=source.at[peer], dst_ref=target.at[emb], send_sem=send_sem, recv_sem=recv_sem,
-                device_id={"emb": peer}, device_id_type=MESH,
-            ).start()
-
-        def send_z(to):
-            for at in places:
-                send(at * nz + to)
-
-        around(z_at, nz, send_z)
-        for at in places:
-            if at is not x_all[0]:
-                send(at * nz + z_at)
-
-    def blocks(value):
-        half = value.shape[1] // 2
-        left = value[:, :half].reshape(nz, CAP, half)
-        right = value[:, half:].reshape(nz, CAP, half)
-        return jnp.concatenate([left, right], axis=1).astype(BF16)
-
-    def together(value):
-        return jnp.concatenate([blocks(value[at * lanes:(at + 1) * lanes]) for at in range(nx)], axis=0)
-
-    def unblocks(value):
-        half = value.shape[2]
-        value = value.astype(F32)
-        left = value[:, :CAP].reshape(groups * CAP, half)
-        right = value[:, CAP:].reshape(groups * CAP, half)
-        return jnp.concatenate([left, right], axis=1).astype(BF16)
-
-    loads[3].wait()
-
-    def answer(at):
-        asked = to_col(fin_ref[at])
-        pick = (asked == (iota((lanes, rows), 1) + 1).astype(F32)).astype(BF16)
-        send_ref[pl.ds(at * nz, nz)] = blocks(dot(pick, table_ref[...]))
-
-    answer(x_at)
-    send_all(x_all[:1], send_ref, recv_ref, rs_sem, rr_sem)
-    finish(fin_ref, nx - 1, xr_sem)
-    for at in x_all[1:]:
-        answer(at)
-    send_all(x_all[1:], send_ref, recv_ref, rs_sem, rr_sem)
-    recv_ref[emb] = send_ref[emb]
-
-    place_ref[...] = (to_col(target) == iota((tokens, groups * CAP), 1).astype(F32)).astype(BF16)
-    at_slot = iota((groups * CAP, tokens), 0).astype(F32)
-    back_ref[...] = (at_slot == target).astype(BF16)
-    for which in range(2):
-        pback_ref[which] = (at_slot == served[which] * CAP + slot).astype(BF16)
-    at_row = (iota((rows, groups * CAP), 0) + 1).astype(F32)
-    put_ref[...] = (at_row == jnp.concatenate([fin_ref[at] for at in range(nx)], axis=1)).astype(BF16)
-    finish(pfin_ref, nx - 1, qr_sem)
-    for which in range(2):
-        asked = jnp.concatenate([pfin_ref[at][which:which + 1] for at in range(nx)], axis=1)
-        pput_ref[which] = (at_row == asked).astype(BF16)
-
-    finish(recv_ref, groups - 1, rr_sem)
-    x_ref[...] = dot(place_ref[...], unblocks(recv_ref[...])).astype(BF16)
-
-    for index in (2, 4, 5, 6):
-        loads[index].wait()
-    forward_backward(seg_ref[...].astype(F32), x_ref, grad_ref, win_ref, wout_ref, gated_ref, dx_ref,
-                     proj_ref, slope_ref, weight_ref, wslope_ref, dz_ref)
-
     part = width // 2
     quarter = part // 2
-    gsend_ref[...] = together(dot(back_ref[...], dx_ref[:, :part]))
+
+    def d_x(cols):
+        value = dot(dz_ref[...], wint_ref[:, cols]).astype(BF16).astype(F32)
+        return (value + grad_ref[:, cols].astype(F32)).astype(BF16)
+
+    gsend_ref[...] = together(dot(back_ref[...], d_x(slice(0, part))))
     send_all(x_all, gsend_ref, grecv_ref, gs_sem, gr_sem)
     grecv_ref[emb] = gsend_ref[emb]
 
-    given = [dot(pback_ref[which], dx_ref[:, part + which * quarter:][:, :quarter]) for which in range(2)]
+    right = d_x(slice(part, width))
+    given = [dot(pback_ref[which], right[:, which * quarter:(which + 1) * quarter]) for which in range(2)]
     psend_ref[...] = together(jnp.concatenate(given, axis=1))
     for peer, k in plane + [(dp, k_at)]:
         for at in x_all:
@@ -347,6 +351,11 @@
 
     mixed_ref[...] = (dot(gated_ref[...], wout_ref[...]) + x_ref[...].astype(F32)).astype(BF16)
 
+    finish(pfin_ref, nx - 1, qr_sem)
+    at_row = (iota((rows, groups * CAP), 0) + 1).astype(F32)
+    for which in range(2):
+        asked = jnp.concatenate([pfin_ref[at][which:which + 1] for at in range(nx)], axis=1)
+        pput_ref[which] = (at_row == asked).astype(BF16)
     finish(precv_ref, groups - 1, hr_sem)
     taken = unblocks(precv_ref[...])
     for which in range(2):
@@ -455,7 +464,9 @@
             pltpu.VMEM((groups, 2 * CAP, width // 2), BF16),
             pltpu.VMEM((tokens, width), BF16),
             pltpu.VMEM((tokens, width), BF16),
+            pltpu.VMEM((tokens, tokens), F32),
             pltpu.VMEM((tokens, width), BF16),
+            pltpu.VMEM((4 * width, width), BF16),
             pltpu.VMEM((tokens, 4 * width), BF16),
             pltpu.VMEM((tokens, 4 * width), F32),
             pltpu.VMEM((pairs, 2 * tokens, tokens), BF16),

time: 93.3 us -> 92.1 us (0.987)
  Pallas kernels: 91.2 us -> 90 us
    pallas_call x1, Pallas kernels: 91.2 us -> 90 us  [layer(): pl.pallas_call(functools.partial(kernel, nx, nz, nd), out_shape=(pltpu.VM...]
where the time goes in v4:
time: 92.1 us; the launch traced here: 92 us
  Pallas kernels  90 us (98%)
  local copies, waits for them, and re-layouts  1.33 us (1%)
    pallas_call x1, Pallas kernels, layer(): pl.pallas_call(functools.partial(kernel, nx, nz, nd), out_shape=(pltpu.VM...  90 us

profile of v4, /device:TPU:1, one launch (start us, length us, event | category | flops | bytes accessed | tf_op | source)
XLA Modules:
  0.0 92.0 jit_solution(15291020489249384543)
XLA Ops:
  0.6 90.0 %hstu.1 = (bf16[256,512]{1,0:T(8,128)(2,1)S(1)}, f32[32,512]{1,0:T(8,128)S(1)}) custom-call(s32[1,256]{1,0:T(1,128)} %bitcast.2, s32[1,256]{1,0:T(1,128)} %bitcast.3, s32[1,256]{1,0:T(1,128)} %seg_hbm.1, bf16[512,512]{1,0:T(8,128)(2,1)} %table_hbm.1, bf16[256,512]{1,0:T(8,128)(2,1)} %grad_hbm.1, bf16[512,2048]{1,0:T(8,128)(2,1)} %win_hbm.1, ...), custom_call_target="tpu_custom_call" | custom-call | tf_op jit(solution)/shard_map/hstu/pallas_call | solution.py:434
  90.7 0.7 copy.11
  91.4 0.6 copy.12

commit v5 on v4

--- a/solution.py
+++ b/solution.py
@@ -69,16 +69,16 @@
         proj_ref[:, part(index)] = act.astype(BF16)
         slope_ref[:, part(index)] = sig + act * (1.0 - sig)
 
-    factor = factor_ref[...]
-    factor = jnp.concatenate([factor, factor], axis=0)
-    first = iota((tokens, lanes), 1) < lanes // 2
+    middle = tokens // 2
+    spans = [(slice(0, middle), middle, slice(tokens, 2 * tokens)), (slice(middle, tokens), tokens, slice(0, tokens))]
+    first = iota((middle, lanes), 1) < lanes // 2
 
     def stack(value):
         zero = jnp.zeros_like(value)
         return jnp.concatenate([jnp.where(first, value, zero), jnp.where(first, zero, value)], axis=0)
 
     def unstack(value):
-        return jnp.where(first, value[:tokens], value[tokens:])
+        return jnp.where(first, value[:middle], value[middle:])
 
     def pair(index, which):
         start = which * width + index * lanes
@@ -86,14 +86,19 @@
 
     attended = []
     for index in range(pairs):
-        q = stack(proj_ref[:, pair(index, 2)])
-        s = dot(q, proj_ref[:, pair(index, 3)], (1, 1)) * scale
-        sig = sigmoid(s)
-        act = s * sig
-        weights = (act * factor).astype(BF16)
-        weight_ref[index] = weights
-        wslope_ref[index] = (sig + act * (1.0 - sig)) * (factor * scale)
-        attended.append(unstack(dot(weights, proj_ref[:, pair(index, 1)])))
+        seen = []
+        for span, keys, at in spans:
+            q = stack(proj_ref[span, pair(index, 2)])
+            s = dot(q, proj_ref[:keys, pair(index, 3)], (1, 1)) * scale
+            sig = sigmoid(s)
+            act = s * sig
+            factor = factor_ref[span, :keys]
+            factor = jnp.concatenate([factor, factor], axis=0)
+            weights = (act * factor).astype(BF16)
+            weight_ref[index, at, :keys] = weights
+            wslope_ref[index, at, :keys] = (sig + act * (1.0 - sig)) * (factor * scale)
+            seen.append(unstack(dot(weights, proj_ref[:keys, pair(index, 1)])))
+        attended.append(jnp.concatenate(seen, axis=0))
     attended = jnp.concatenate(attended, axis=1)
 
     center = attended - jnp.mean(attended, axis=1, keepdims=True)
@@ -117,14 +122,22 @@
         value = value.astype(BF16).astype(F32)
         dz_ref[:, pair(index, which)] = (value * slope_ref[:, pair(index, which)]).astype(BF16)
 
+    def whole(early, late):
+        return jnp.concatenate([early + late[:middle], late[middle:]], axis=0)
+
     for index in range(pairs):
-        q = stack(proj_ref[:, pair(index, 2)])
-        d = stack(d_att[:, index * lanes:(index + 1) * lanes])
-        put(index, 1, dot(weight_ref[index], d, (0, 0)))
-        d_s = dot(d, proj_ref[:, pair(index, 1)], (1, 1)) * wslope_ref[index]
-        d_s = d_s.astype(BF16)
-        put(index, 2, unstack(dot(d_s, proj_ref[:, pair(index, 3)])))
-        put(index, 3, dot(d_s, q, (0, 0)))
+        d_v, d_q, d_k = [], [], []
+        for span, keys, at in spans:
+            q = stack(proj_ref[span, pair(index, 2)])
+            d = stack(d_att[span, index * lanes:(index + 1) * lanes])
+            d_v.append(dot(weight_ref[index, at, :keys], d, (0, 0)))
+            d_s = dot(d, proj_ref[:keys, pair(index, 1)], (1, 1)) * wslope_ref[index, at, :keys]
+            d_s = d_s.astype(BF16)
+            d_q.append(unstack(dot(d_s, proj_ref[:keys, pair(index, 3)])))
+            d_k.append(dot(d_s, q, (0, 0)))
+        put(index, 1, whole(*d_v))
+        put(index, 2, jnp.concatenate(d_q, axis=0))
+        put(index, 3, whole(*d_k))
 
 
 def kernel(nx, nz, nd,

time: 92.1 us -> 92 us (level)
  no operation moved by 1% of the time
where the time goes in v5:
time: 92 us; the launch traced here: 91.8 us
  Pallas kernels  89.9 us (98%)
  local copies, waits for them, and re-layouts  1.33 us (1%)
    pallas_call x1, Pallas kernels, layer(): pl.pallas_call(functools.partial(kernel, nx, nz, nd), out_shape=(pltpu.VM...  89.9 us

profile of v5, /device:TPU:1, one launch (start us, length us, event | category | flops | bytes accessed | tf_op | source)
XLA Modules:
  0.0 91.8 jit_solution(3340848291029075697)
XLA Ops:
  0.6 89.9 %hstu.1 = (bf16[256,512]{1,0:T(8,128)(2,1)S(1)}, f32[32,512]{1,0:T(8,128)S(1)}) custom-call(s32[1,256]{1,0:T(1,128)} %bitcast.2, s32[1,256]{1,0:T(1,128)} %bitcast.3, s32[1,256]{1,0:T(1,128)} %seg_hbm.1, bf16[512,512]{1,0:T(8,128)(2,1)} %table_hbm.1, bf16[256,512]{1,0:T(8,128)(2,1)} %grad_hbm.1, bf16[512,2048]{1,0:T(8,128)(2,1)} %win_hbm.1, ...), custom_call_target="tpu_custom_call" | custom-call | tf_op jit(solution)/shard_map/hstu/pallas_call | solution.py:447
  90.5 0.7 copy.11
  91.2 0.6 copy.12
